TPU v7x, 512 devices: a whole 4x8x8 slice. The times are simulated.
512 devices in a mesh: sec: 8 (over z_hi, x), gy: 8 (over z_lo, core), gx: 8 (over y).
Axes of the slice: x: 4, y: 8, z: 8 (z_hi: 2, z_lo: 4; z = z_hi * 4 + z_lo), core: 2. Of those that a mesh axis runs over, the one named last changes fastest.
Arguments:
- images: bfloat16 [64, 64, 1024], P(('sec', 'gy'), None, 'gx'), may hold values from -6 to 6
- offsets: int32 [64, 8, 2, 8], P(('sec', 'gy'), None, None, 'gx'), may hold values from 0 to 4, as said below
- stem_kernel: bfloat16 [32, 1, 1, 3, 3], replicated, may hold values from -2 to 2
- stem_bias: float32 [32], replicated, may hold values from -3 to 3
- outer_kernel: bfloat16 [32, 32, 1, 3, 3], replicated, may hold values from -0.375 to 0.375
- outer_bias: float32 [32], replicated, may hold values from -3 to 3
- pooling_kernel: bfloat16 [64, 32, 1, 2, 2], replicated, may hold values from -0.5 to 0.5
- pooling_bias: float32 [64], replicated, may hold values from -3 to 3
- inner_kernel: bfloat16 [3, 3, 3, 4096], replicated, may hold values from -0.15625 to 0.15625
- inner_bias: float32 [64], replicated, may hold values from -3 to 3
- narrowing_kernel: bfloat16 [128, 64, 1, 2, 2], replicated, may hold values from -0.375 to 0.375
- narrowing_bias: float32 [128], replicated, may hold values from -3 to 3
- bottom_kernel: bfloat16 [3, 3, 3, 16384], replicated, may hold values from -0.109375 to 0.109375
- bottom_bias: float32 [128], replicated, may hold values from -3 to 3
- lift_kernel: bfloat16 [128, 64, 1, 2, 2], replicated, may hold values from -0.5 to 0.5
- lift_bias: float32 [64], replicated, may hold values from -3 to 3
- mend_kernel: bfloat16 [64, 64, 1, 3, 3], replicated, may hold values from -0.25 to 0.25
- mend_bias: float32 [64], replicated, may hold values from -3 to 3
- expand_kernel: bfloat16 [64, 32, 1, 2, 2], replicated, may hold values from -0.75 to 0.75
- expand_bias: float32 [32], replicated, may hold values from -3 to 3
- finish_kernel: bfloat16 [32, 32, 1, 3, 3], replicated, may hold values from -0.375 to 0.375
- finish_bias: float32 [32], replicated, may hold values from -3 to 3
- head_kernel: bfloat16 [3, 32], replicated, may hold values from -1 to 1
- head_bias: float32 [3], replicated, may hold values from -3 to 3
Outputs:
- affinities: float32 [3, 64, 64, 1024], P(None, 'sec', 'gy', 'gx')
Inputs may be any that keep to these rules, and one draw needn't show every extreme that they name: `offsets`: each section has a tile with a shift of exactly 4.
All inputs are finite; a program needn't handle non-finite values.
Results may differ from a plain program's by a relative error of at most 0.025.
Values may be sent and summed in bfloat16 or wider, within the bound.
A program may use at most 64 MiB of HBM per device.

v0:
```python
import functools
import numpy as np
import jax
import jax.numpy as jnp
from jax import lax
from jax.experimental import pallas as pl
from jax.experimental.pallas import tpu as pltpu
from jax.sharding import PartitionSpec as P

BF = jnp.bfloat16
F32 = jnp.float32
PITCH = 40
NZ = 12
R12, R10, R8 = NZ * PITCH, 10 * PITCH, 8 * PITCH
PAD = 16


def stem_table():
    cols = [0, 1, 2, 3, 4, 5, -2, -1]
    outs = [(ro, j) for ro in range(2) for j in range(4)] + [(0, 4), (1, -1), (1, 4), (0, -1)]
    t = np.zeros((8, 4, 12, 3, 3), np.float32)
    for a, i in enumerate(cols):
        for r in range(4):
            for b, (ro, j) in enumerate(outs):
                dy, dx = r - ro, i - j + 1
                if 0 <= dy < 3 and 0 <= dx < 3:
                    t[a, r, b, dy, dx] = 1
    return t


def plane_table(width):
    ks = [(r, i) for r in range(4) for i in range(width)]
    if width == 4:
        for h in range(2):
            ks += [(2 * h, 4), (2 * h + 1, -1), (2 * h + 1, 4), (2 * h, -1)]
    else:
        for r in range(4):
            ks += [(r, 2), (r, -1)]
    outs = [(ro, j) for ro in range(2) for j in range(width)]
    t = np.zeros((len(ks), len(outs), 3, 3), np.float32)
    for a, (r, i) in enumerate(ks):
        for b, (ro, j) in enumerate(outs):
            dy, dx = r - ro, i - j + 1
            if 0 <= dy < 3 and 0 <= dx < 3:
                t[a, b, dy, dx] = 1
    return t


def prep_weights(w):
    d = {}
    base = jnp.einsum("arbyx,oyx->arbo", jnp.asarray(stem_table(), BF), w["stem_kernel"][:, 0, 0]).astype(BF)
    base = base.reshape(8, 4, 384)
    d["stem"] = jnp.stack([jnp.pad(base, ((0, 0), (2 * q, 28 - 2 * q), (0, 0))).reshape(256, 384) for q in range(15)])
    for name, width, ch in (("outer", 4, 32), ("finish", 4, 32), ("mend", 2, 64)):
        t = jnp.asarray(plane_table(width), BF)
        m = jnp.einsum("abyx,ocyx->acbo", t, w[name + "_kernel"][:, :, 0]).astype(BF)
        d[name] = m.reshape(t.shape[0] * ch, 256)
    t = jnp.asarray(plane_table(2), BF)
    kin = w["inner_kernel"].reshape(3, 3, 3, 64, 64)
    d["inner"] = jnp.einsum("abyx,zyxco->zacbo", t, kin).astype(BF).reshape(3, 1024, 256)
    kb = w["bottom_kernel"].reshape(3, 3, 3, 128, 128)
    rows = [[kb[:, r - ro] if 0 <= r - ro < 3 else jnp.zeros_like(kb[:, 0]) for ro in range(2)] for r in range(4)]
    d["bottom"] = jnp.stack([jnp.stack(q, 3) for q in rows], 1).reshape(3, 1536, 256)

    def down(k, width):
        eye = np.zeros((width, width // 2, 2), np.float32)
        for i in range(width):
            eye[i, i // 2, i % 2] = 1
        m = jnp.einsum("ijq,ocpq->picjo", jnp.asarray(eye, BF), k[:, :, 0]).astype(BF)
        return m.reshape(2 * width * k.shape[1], -1)

    def up(k, width):
        eye = np.zeros((width, width // 2, 2), np.float32)
        for i in range(width):
            eye[i, i // 2, i % 2] = 1
        m = jnp.einsum("ijq,copq->jcpio", jnp.asarray(eye, BF), k[:, :, 0]).astype(BF)
        return m.reshape(width // 2 * k.shape[0], -1)

    d["pool"] = down(w["pooling_kernel"], 4)
    d["narrow"] = down(w["narrowing_kernel"], 2)
    d["lift"] = up(w["lift_kernel"], 2)
    d["expand"] = up(w["expand_kernel"], 4)
    hk = w["head_kernel"]
    eye2 = jnp.eye(2, dtype=BF)
    h = jnp.einsum("rs,oc->roscj", eye2, hk)[:, :, :, None, :, 0] if False else None
    head = jnp.einsum("rs,j,oc->rosjc", eye2, jnp.ones((4,), BF), hk).astype(BF).reshape(6, 256)
    d["head"] = jnp.pad(head, ((0, 2), (0, 0)))
    b = {}
    s4 = jnp.tile(w["stem_bias"], 12)
    b["stem"] = s4[None]
    b["outer"] = jnp.tile(w["outer_bias"], 8)[None]
    b["finish"] = jnp.tile(w["finish_bias"], 8)[None]
    b["expand"] = jnp.tile(w["expand_bias"], 8)[None]
    b["pool"] = jnp.tile(w["pooling_bias"], 2)[None]
    b["inner"] = jnp.tile(w["inner_bias"], 4)[None]
    b["mend"] = jnp.tile(w["mend_bias"], 4)[None]
    b["lift"] = jnp.tile(w["lift_bias"], 4)[None]
    b["narrow"] = w["narrowing_bias"][None]
    b["bottom"] = jnp.tile(w["bottom_bias"], 2)[None]
    return d, b


WN = ("stem", "outer", "pool", "inner", "narrow", "bottom", "lift", "mend", "expand", "finish", "head")
BN = ("stem", "outer", "pool", "inner", "narrow", "bottom", "lift", "mend", "expand", "finish")


def dot(a, b):
    return jnp.dot(a, b, preferred_element_type=F32)


def compute(pos, counts, x4, W, B, out, sc):
    sec, gy, gx = pos
    nsec, ngy, ngx = counts
    lane = lax.broadcasted_iota(jnp.int32, (1, 128), 1)
    rows = lax.broadcasted_iota(jnp.int32, (R12, 1), 0)
    zi = rows // PITCH
    gi = rows - zi * PITCH
    zglob = sec * 8 - 2 + zi
    zok = jnp.logical_and(zglob >= 0, zglob < nsec * 8)
    gg = gx * 32 - 3 + gi

    def gok(shift):
        return jnp.logical_and(gg + shift >= 0, gg + shift < ngx * 32)

    m = jnp.broadcast_to(jnp.where(jnp.logical_and(zok, gok(0)), 1.0, 0.0), (R12, 128))
    sc.mask[0] = jnp.zeros((R12, 128), F32)
    sc.mask[1] = m
    sc.smask[0] = jnp.zeros((R12, 128), BF)
    sc.smask[1] = m.astype(BF)
    right = jnp.where(gok(1), 1.0, 0.0)
    left = jnp.where(gok(-1), 1.0, 0.0)
    zero = jnp.zeros((R12, 1), F32)
    for va in range(2):
        for vb in range(2):
            ra, la = (right, left) if va else (zero, zero)
            rb, lb = (right, left) if vb else (zero, zero)
            e = jnp.where(lane < 32, ra, jnp.where(lane < 64, lb, jnp.where(lane < 96, rb, la)))
            sc.emask[2 * va + vb] = e.astype(BF)

    def rowok(row, total):
        return jnp.where(jnp.logical_and(row >= 0, row < total), 1, 0)

    sc.xf[0:PAD] = jnp.zeros((PAD, 128), F32)
    sc.xf[PAD + R12 :] = jnp.zeros((PAD, 128), F32)
    for z in range(NZ):
        sc.xf[PAD + z * PITCH : PAD + (z + 1) * PITCH] = x4[z, 0:PITCH].astype(F32)
    sc.xin[:, 0:128] = sc.xf[PAD : PAD + R12].astype(BF)
    sc.xin[:, 128:256] = jnp.where(
        lane < 64, sc.xf[PAD + 1 : PAD + 1 + R12], sc.xf[PAD - 1 : PAD - 1 + R12]
    ).astype(BF)

    def stem(q, _):
        acc = dot(sc.xin[...], W["stem"][q]) + B["stem"][...]
        s = acc.astype(BF)
        va = rowok(gy * 8 + 2 * q - 11, ngy * 8)
        vb = rowok(gy * 8 + 2 * q - 10, ngy * 8)
        sc.s[2 * q] = s[:, 0:128]
        sc.s[2 * q + 1] = s[:, 128:256]
        r = jnp.maximum(s, jnp.zeros((), BF))
        sc.r[2 * q] = r[:, 0:128] * sc.smask[va]
        sc.r[2 * q + 1] = r[:, 128:256] * sc.smask[vb]
        sc.e[q] = r[:, 256:384] * sc.emask[2 * va + vb]
        return 0

    lax.fori_loop(0, 15, stem, 0)

    sc.pf[:, 0:PAD] = jnp.zeros((14, PAD, 128), F32)
    sc.pf[:, PAD + R12 :] = jnp.zeros((14, PAD, 128), F32)

    def outer(p, _):
        lhs = jnp.concatenate(
            [sc.r[2 * p], sc.r[2 * p + 1], sc.r[2 * p + 2], sc.r[2 * p + 3], sc.e[p], sc.e[p + 1]], axis=1
        )
        acc = dot(lhs, W["outer"][...])
        res = jnp.concatenate([sc.s[2 * p + 1], sc.s[2 * p + 2]], axis=1).astype(F32)
        o = (acc + res + B["outer"][...]).astype(BF)

        sc.o[p] = o[80:400]
        pooled = (dot(o, W["pool"][...]) + B["pool"][...]).astype(BF).astype(F32)
        v = rowok(gy * 4 + p - 5, ngy * 4)
        pooled = pooled * sc.mask[v]
        sc.pf[p, PAD : PAD + R12] = pooled
        sc.pa[p, :, 0:128] = jnp.maximum(pooled, 0.0).astype(BF)
        ea = jnp.where(lane < 64, sc.pf[p, PAD + 1 : PAD + 1 + R12], sc.pf[p, PAD - 1 : PAD - 1 + R12])
        sc.pa[p, :, 128:256] = jnp.maximum(ea, 0.0).astype(BF)
        sc.pb[p, :, 0:128] = jnp.maximum(sc.pf[p, PAD - 8 : PAD + 8 + R12], 0.0).astype(BF)
        eb = jnp.where(lane < 64, sc.pf[p, PAD - 7 : PAD + 9 + R12], sc.pf[p, PAD - 9 : PAD + 7 + R12])
        sc.pb[p, :, 128:256] = jnp.maximum(eb, 0.0).astype(BF)
        return 0

    lax.fori_loop(0, 14, outer, 0)

    sc.qf[:, 0:PAD] = jnp.zeros((6, PAD, 128), F32)
    sc.qf[:, PAD + R10 :] = jnp.zeros((6, PAD, 128), F32)

    def inner(k, _):
        acc = jnp.zeros((R10, 256), F32)
        for dz in range(3):
            src = (sc.pa, sc.pb, sc.pa)[dz]
            lo = (0, 48, 80)[dz]
            lhs = jnp.concatenate(
                [src[2 * k + r, lo : lo + R10, 0:128] for r in range(4)]
                + [src[2 * k + r, lo : lo + R10, 128:256] for r in range(4)],
                axis=1,
            )
            acc = acc + dot(lhs, W["inner"][dz])
        res = jnp.concatenate(
            [sc.pf[2 * k + 1, PAD + 40 : PAD + 440], sc.pf[2 * k + 2, PAD + 40 : PAD + 440]], axis=1
        )
        a = (acc + res + B["inner"][...]).astype(BF)
        sc.i[k] = a.astype(F32)[40:360].astype(BF)
        sq = (dot(a, W["narrow"][...]) + B["narrow"][...]).astype(BF).astype(F32)
        v = rowok(gy * 2 + k - 2, ngy * 2)
        sq = sq * sc.mask[v, 40:440]
        sc.qf[k, PAD : PAD + R10] = sq
        for d in range(3):
            sc.qa[k, :, d * 128 : (d + 1) * 128] = jnp.maximum(
                sc.qf[k, PAD - 1 + d : PAD - 1 + d + R10], 0.0
            ).astype(BF)
            sc.qb[k, :, d * 128 : (d + 1) * 128] = jnp.maximum(
                sc.qf[k, PAD - 9 + d : PAD + 7 + d + R10], 0.0
            ).astype(BF)
        return 0

    lax.fori_loop(0, 6, inner, 0)

    sc.lf[:, 0:PAD] = jnp.zeros((8, PAD, 128), F32)
    sc.lf[:, PAD + R8 :] = jnp.zeros((8, PAD, 128), F32)

    def bottom(mi, _):
        acc = jnp.zeros((R8, 256), F32)
        for dz in range(3):
            src = (sc.qa, sc.qb, sc.qa)[dz]
            lo = (0, 48, 80)[dz]
            lhs = jnp.concatenate([src[2 * mi + r, lo : lo + R8, :] for r in range(4)], axis=1)
            acc = acc + dot(lhs, W["bottom"][dz])
        res = jnp.concatenate(
            [sc.qf[2 * mi + 1, PAD + 40 : PAD + 360], sc.qf[2 * mi + 2, PAD + 40 : PAD + 360]], axis=1
        )
        a = (acc + res + B["bottom"][...]).astype(BF)
        for h in range(2):
            up = dot(a[:, h * 128 : (h + 1) * 128], W["lift"][...])
            y = 2 * mi + h
            l = (up + sc.i[y + 1].astype(F32) + B["lift"][...]).astype(BF).astype(F32)
            for e in range(2):
                t = 2 * y + e
                v = rowok(gy * 4 + t - 2, ngy * 4)
                lm = l[:, e * 128 : (e + 1) * 128] * sc.mask[v, 80:400]
                sc.lf[t, PAD : PAD + R8] = lm
                sc.la[t, :, 0:128] = jnp.maximum(lm, 0.0).astype(BF)
                ed = jnp.where(lane < 64, sc.lf[t, PAD + 1 : PAD + 1 + R8], sc.lf[t, PAD - 1 : PAD - 1 + R8])
                sc.la[t, :, 128:256] = jnp.maximum(ed, 0.0).astype(BF)
        return 0

    lax.fori_loop(0, 2, bottom, 0)

    sc.ef[:, 0:PAD] = jnp.zeros((12, PAD, 128), F32)
    sc.ef[:, PAD + R8 :] = jnp.zeros((12, PAD, 128), F32)

    def mend(n, _):
        lhs = jnp.concatenate(
            [sc.la[2 * n + r, :, 0:128] for r in range(4)] + [sc.la[2 * n + r, :, 128:256] for r in range(4)],
            axis=1,
        )
        acc = dot(lhs, W["mend"][...])
        res = jnp.concatenate(
            [sc.lf[2 * n + 1, PAD : PAD + R8], sc.lf[2 * n + 2, PAD : PAD + R8]], axis=1
        )
        a = (acc + res + B["mend"][...]).astype(BF)
        for h in range(2):
            j = 2 * n + h
            up = dot(a[:, h * 128 : (h + 1) * 128], W["expand"][...])
            x = (up + sc.o[4 + j].astype(F32) + B["expand"][...]).astype(BF).astype(F32)
            for e in range(2):
                t = 2 * j + e
                v = rowok(gy * 8 + t - 2, ngy * 8)
                xm = x[:, e * 128 : (e + 1) * 128] * sc.mask[v, 80:400]
                sc.ef[t, PAD : PAD + R8] = xm
                sc.ea[t] = jnp.maximum(xm, 0.0).astype(BF)
        return 0

    lax.fori_loop(0, 3, mend, 0)

    def edges(u, _):
        ta, tb = 2 * u + 1, 2 * u + 2
        ua = jnp.where(lane < 64, sc.ef[ta, PAD + 1 : PAD + 1 + R8], sc.ef[ta, PAD - 1 : PAD - 1 + R8])
        ub = jnp.where(lane < 64, sc.ef[tb, PAD + 1 : PAD + 1 + R8], sc.ef[tb, PAD - 1 : PAD - 1 + R8])
        ub = pltpu.roll(ub, 64, 1)
        e = jnp.where(jnp.logical_and(lane >= 32, lane < 96), ub, ua)
        sc.ee[u] = jnp.maximum(e, 0.0).astype(BF)
        return 0

    lax.fori_loop(0, 5, edges, 0)

    lane2 = lax.broadcasted_iota(jnp.int32, (1, 256), 1)
    jl = (lane2 // 32) % 4

    def finish(u, _):
        lhs = jnp.concatenate(
            [sc.ea[2 * u + 1 + r] for r in range(4)] + [sc.ee[u], sc.ee[u + 1]], axis=1
        )
        acc = dot(lhs, W["finish"][...])
        res = jnp.concatenate(
            [sc.ef[2 * u + 2, PAD : PAD + R8], sc.ef[2 * u + 3, PAD : PAD + R8]], axis=1
        )
        f = (acc + res + B["finish"][...]).astype(BF).astype(F32)
        sc.f[0:R8, 0] = f[:, 0:128]
        sc.f[0:R8, 1] = f[:, 128:256]
        return 0

    def finish2(u, _):
        lhs = jnp.concatenate(
            [sc.ea[2 * u + 1 + r] for r in range(4)] + [sc.ee[u], sc.ee[u + 1]], axis=1
        )
        acc = dot(lhs, W["finish"][...])
        res = jnp.concatenate(
            [sc.ef[2 * u + 2, PAD : PAD + R8], sc.ef[2 * u + 3, PAD : PAD + R8]], axis=1
        )
        f = (acc + res + B["finish"][...]).astype(BF).astype(F32)
        for h in range(2):
            sc.f[h, 0:R8] = f[:, h * 128 : (h + 1) * 128]
        for h in range(2):
            for z in range(8):
                fz = sc.f[h, z * PITCH + 3 : z * PITCH + 35]
                for j in range(4):
                    sc.g[h, pl.ds(z * 128 + j, 32, 4), :] = jnp.where(lane // 32 == j, fz, 0.0)
        for z in range(8):
            gz = jnp.concatenate([sc.g[h, z * 128 : (z + 1) * 128] for h in range(2)], axis=1).astype(BF)
            lt = lax.dot_general(W["head"][...], gz, (((1,), (1,)), ((), ())), preferred_element_type=F32)
            for ro in range(2):
                for o in range(3):
                    out[o, z, pl.ds(2 * u + ro, 1), :] = lt[ro * 3 + o : ro * 3 + o + 1]
        return 0

    lax.fori_loop(0, 4, finish2, 0)


SCRATCH = dict(
    mask=((2, R12, 128), F32),
    smask=((2, R12, 128), BF),
    emask=((4, R12, 128), BF),
    xf=((R12 + 2 * PAD, 128), F32),
    xin=((R12, 256), BF),
    s=((30, R12, 128), BF),
    r=((30, R12, 128), BF),
    e=((15, R12, 128), BF),
    o=((14, R8, 256), BF),
    pf=((14, R12 + 2 * PAD, 128), F32),
    pa=((14, R12, 256), BF),
    pb=((14, R12 + 16, 256), BF),
    i=((6, R8, 256), BF),
    qf=((6, R10 + 2 * PAD, 128), F32),
    qa=((6, R10, 384), BF),
    qb=((6, R10 + 16, 384), BF),
    lf=((8, R8 + 2 * PAD, 128), F32),
    la=((8, R8, 256), BF),
    ef=((12, R8 + 2 * PAD, 128), F32),
    ea=((12, R8, 128), BF),
    ee=((5, R8, 128), BF),
    f=((2, R8, 128), F32),
    g=((2, 1024, 128), F32),
)


class Refs:
    def __init__(self, names, refs):
        for n, r in zip(names, refs):
            setattr(self, n, r)


def unet_call(pos_fn, counts, x4, d, b, interpret=False):
    def body(*refs):
        x4r = refs[0]
        n = 1
        W = dict(zip(WN, refs[n : n + len(WN)]))
        n += len(WN)
        B = dict(zip(BN, refs[n : n + len(BN)]))
        n += len(BN)
        out = refs[n]
        sc = Refs(SCRATCH, refs[n + 1 :])
        compute(pos_fn(), counts, x4r, W, B, out, sc)

    vm = pl.BlockSpec(memory_space=pltpu.VMEM)
    return pl.pallas_call(
        body,
        out_shape=jax.ShapeDtypeStruct((3, 8, 8, 128), F32),
        in_specs=[vm] * (1 + len(WN) + len(BN)),
        out_specs=vm,
        scratch_shapes=[pltpu.VMEM(s, t) for s, t in SCRATCH.values()],
        compiler_params=pltpu.CompilerParams(vmem_limit_bytes=60 * 1024 * 1024),
        interpret=interpret,
    )(x4, *[d[k] for k in WN], *[b[k] for k in BN])
MESH = pl.DeviceIdType.MESH


def axis_position():
    return lax.axis_index("sec"), lax.axis_index("gy"), lax.axis_index("gx")


def align(own, left, right, off, has_left, has_right, cs):
    lane = lax.broadcasted_iota(jnp.int32, (1, 128), 1)

    def shifts(ref, first, ok):
        v = ref[64:80].astype(F32)
        m = jnp.concatenate([jnp.broadcast_to(v[first + i : first + i + 1], (8, 128)) for i in range(8)], axis=0)
        return m if ok is None else jnp.where(ok, m, -1.0)

    pix = [r[0:64].astype(F32) for r in (left, own, right)]
    oy = [shifts(left, 0, has_left), shifts(own, 0, None), shifts(right, 0, has_right)]
    ox = [shifts(left, 8, has_left), shifts(own, 8, None), shifts(right, 8, has_right)]
    rp = [pltpu.roll(p, 16, 1) for p in pix]
    for tile in range(2):
        raw = jnp.where(lane < 16, rp[tile], rp[tile + 1])
        oyt = jnp.where(lane < 16, oy[tile], oy[tile + 1])
        oxt = jnp.where(lane < 16, ox[tile], ox[tile + 1])
        for s in range(5):
            hit = oxt == float(s)
            v = jnp.where(hit, raw, 0.0)
            o = jnp.where(hit, oyt, -1.0)
            cs.vs[s, tile] = v if s == 0 else pltpu.roll(v, s, 1)
            cs.os[s, tile] = o if s == 0 else pltpu.roll(o, s, 1)
    cs.vb[:, :, 0:8] = jnp.zeros((2, 2, 8, 128), F32)
    for tile in range(2):
        total = jnp.zeros((64, 128), F32)
        cover = jnp.zeros((64, 128), F32)
        for t in range(5):
            v = jnp.zeros((64, 128), F32)
            c = jnp.zeros((64, 128), F32)
            for s in range(5):
                vs, os = cs.vs[s, tile], cs.os[s, tile]
                if tile == 1 and s > 0:
                    vs = jnp.where(lane < s, cs.vs[s, 0], vs)
                    os = jnp.where(lane < s, cs.os[s, 0], os)
                hit = os == float(t)
                v = v + jnp.where(hit, vs, 0.0)
                c = c + jnp.where(hit, 1.0, 0.0)
            if t > 0:
                cs.vb[tile, 0, 8:72] = v
                cs.vb[tile, 1, 8:72] = c
                v = cs.vb[tile, 0, 8 - t : 72 - t]
                c = cs.vb[tile, 1, 8 - t : 72 - t]
            total = total + v
            cover = cover + c
        a = (total / jnp.maximum(cover, 1.0)).astype(BF).astype(F32)
        if tile == 0:
            a = jnp.where(jnp.logical_or(lane >= 16, has_left), a, 0.0)
        else:
            a = jnp.where(jnp.logical_or(lane < 16, has_right), a, 0.0)
        a = jnp.concatenate([a, jnp.zeros((64, 128), F32)], axis=0)
        cs.tt[tile * 128 : (tile + 1) * 128] = a.T
    xs = [cs.tt[pl.ds(4 + i, 48, 4), :] for i in range(4)]
    for g in range(8):
        piece = jnp.zeros((48, 128), F32)
        for i in range(4):
            sh = (32 * i - (8 * g - 12)) % 128
            r = xs[i] if sh == 0 else pltpu.roll(xs[i], sh, 1)
            piece = jnp.where(lane // 32 == i, r, piece)
        cs.sbuf[g] = piece.astype(BF)


CS = dict(
    near=((80, 128), BF),
    rb=((2, 80, 128), BF),
    sbuf=((8, 48, 128), BF),
    rx=((NZ, 48, 128), BF),
    vs=((5, 2, 64, 128), F32),
    os=((5, 2, 64, 128), F32),
    vb=((2, 2, 72, 128), F32),
    tt=((256, 128), F32),
)


def gather(img, off, cs, sems, counts):
    send1, recv1, send2, send3, recv2 = sems
    sec, gy, gx = axis_position()
    nsec, ngy, ngx = counts
    one = jnp.int32(1)
    has_left, has_right = gx > 0, gx < ngx - 1
    above, below = sec > 0, sec < nsec - 1
    barrier = pltpu.get_barrier_semaphore()

    def greet(*device):
        pl.semaphore_signal(barrier, inc=1, device_id=device, device_id_type=MESH)

    cs.rx[...] = jnp.zeros((NZ, 48, 128), BF)
    cs.rb[...] = jnp.zeros((2, 80, 128), BF)

    @pl.when(has_left)
    def _():
        greet(sec, gy, gx - 1)

    @pl.when(has_right)
    def _():
        greet(sec, gy, gx + 1)

    for k in range(1, 8):
        greet(sec, lax.rem(gy + k, 8), gx)

    @pl.when(below)
    def _():
        greet(sec + 1, 0 * gy, gx)
        greet(sec + 1, 0 * gy + 1, gx)

    @pl.when(above)
    def _():
        greet(sec - 1, 0 * gy + 6, gx)
        greet(sec - 1, 0 * gy + 7, gx)

    to_up = jnp.logical_and(gy < 2, above)
    to_down = jnp.logical_and(gy >= 6, below)
    expect = 7 + jnp.where(has_left, 1, 0) + jnp.where(has_right, 1, 0) + jnp.where(jnp.logical_or(to_up, to_down), 8, 0)

    cs.near[0:64] = img[...]
    r16 = lax.broadcasted_iota(jnp.int32, (16, 128), 0)
    info = jnp.zeros((16, 128), F32)
    for i in range(8):
        info = jnp.where(r16 == i, off[i, 0].astype(F32), info)
        info = jnp.where(r16 == 8 + i, off[i, 1].astype(F32), info)
    cs.near[64:80] = info.astype(BF)

    pl.semaphore_wait(barrier, expect)

    def near_copy(slot, target):
        return pltpu.make_async_remote_copy(
            src_ref=cs.near, dst_ref=cs.rb.at[slot], send_sem=send1.at[slot], recv_sem=recv1.at[slot],
            device_id=(sec, gy, target), device_id_type=MESH,
        )

    @pl.when(has_right)
    def _():
        near_copy(0, gx + 1).start()

    @pl.when(has_left)
    def _():
        near_copy(1, gx - 1).start()

    @pl.when(has_left)
    def _():
        near_copy(0, gx - 1).wait_recv()

    @pl.when(has_right)
    def _():
        near_copy(1, gx + 1).wait_recv()

    align(cs.near, cs.rb.at[0], cs.rb.at[1], off, has_left, has_right, cs)

    def far(g, slot, s, sem):
        return pltpu.make_async_remote_copy(
            src_ref=cs.sbuf.at[g], dst_ref=cs.rx.at[slot], send_sem=sem.at[g], recv_sem=recv2.at[slot],
            device_id=(s, g, gx), device_id_type=MESH,
        )

    for k in range(1, 8):
        far(lax.rem(gy + k, 8), gy + 2, sec, send2).start()

    @pl.when(to_up)
    def _():
        for k in range(8):
            far(lax.rem(gy + k, 8), gy + 10, sec - 1, send3).start()

    @pl.when(to_down)
    def _():
        for k in range(8):
            far(lax.rem(gy + k, 8), gy - 6, sec + 1, send3).start()

    cs.rx[gy + 2] = cs.sbuf[gy]

    def finish():
        for k in range(1, 8):
            far(lax.rem(gy + k, 8), 2 + lax.rem(gy + k, 8), sec, send2).wait_recv()

        @pl.when(above)
        def _():
            for slot in (0, 1):
                far(lax.rem(gy + 1, 8), slot, sec - 1, send3).wait_recv()

        @pl.when(below)
        def _():
            for slot in (10, 11):
                far(lax.rem(gy + 1, 8), slot, sec + 1, send3).wait_recv()

    def drain():
        @pl.when(has_right)
        def _():
            near_copy(0, gx + 1).wait_send()

        @pl.when(has_left)
        def _():
            near_copy(1, gx - 1).wait_send()

        for k in range(1, 8):
            far(lax.rem(gy + k, 8), gy + 2, sec, send2).wait_send()

        @pl.when(to_up)
        def _():
            for k in range(8):
                far(lax.rem(gy + k, 8), gy + 10, sec - 1, send3).wait_send()

        @pl.when(to_down)
        def _():
            for k in range(8):
                far(lax.rem(gy + k, 8), gy - 6, sec + 1, send3).wait_send()

    return finish, drain


def gather_call(images, offsets, counts):
    def body(img, off, out, *rest):
        cs = Refs(CS, rest[: len(CS)])
        finish, drain = gather(img, off, cs, rest[len(CS) :], counts)
        finish()
        drain()
        out[...] = cs.rx[...]

    dma = pltpu.SemaphoreType.DMA
    return pl.pallas_call(
        body,
        out_shape=jax.ShapeDtypeStruct((NZ, 48, 128), BF),
        in_specs=[pl.BlockSpec(memory_space=pltpu.VMEM), pl.BlockSpec(memory_space=pltpu.SMEM)],
        out_specs=pl.BlockSpec(memory_space=pltpu.VMEM),
        scratch_shapes=[pltpu.VMEM(s, t) for s, t in CS.values()]
        + [dma((2,)), dma((2,)), dma((8,)), dma((8,)), dma((12,))],
        compiler_params=pltpu.CompilerParams(
            vmem_limit_bytes=24 * 1024 * 1024, collective_id=0, has_side_effects=True
        ),
    )(images, offsets)


NAMES = (
    "images", "offsets", "stem_kernel", "stem_bias", "outer_kernel", "outer_bias", "pooling_kernel",
    "pooling_bias", "inner_kernel", "inner_bias", "narrowing_kernel", "narrowing_bias", "bottom_kernel",
    "bottom_bias", "lift_kernel", "lift_bias", "mend_kernel", "mend_bias", "expand_kernel", "expand_bias",
    "finish_kernel", "finish_bias", "head_kernel", "head_bias",
)


def solution(mesh):
    counts = (mesh.shape["sec"], mesh.shape["gy"], mesh.shape["gx"])

    def per_device(*args):
        w = dict(zip(NAMES, args))
        x4 = gather_call(w["images"].reshape(64, 128), w["offsets"].reshape(8, 2), counts)
        d, b = prep_weights(w)
        logits = unet_call(axis_position, counts, x4, d, b)
        return jax.nn.sigmoid(logits + w["head_bias"][:, None, None, None])

    in_specs = (P(("sec", "gy"), None, "gx"), P(("sec", "gy"), None, None, "gx")) + (P(),) * 22
    out_specs = P(None, "sec", "gy", "gx")
    return jax.shard_map(per_device, mesh=mesh, in_specs=in_specs, out_specs=out_specs, check_vma=False)
```

profile of v0, /device:TPU:31, one launch (start us, length us, event | category | flops | bytes accessed | tf_op | source)
XLA Modules:
  0.0 104.7 jit_solution(11583838744929052510)
XLA Ops:
  0.0 0.8 copy.54.off
  0.8 0.7 copy-done.2
  1.5 21.9 %shard_map.307.refs_0_ = bf16[12,48,128]{2,1,0:T(8,128)(2,1)S(1)} custom-call(bf16[64,128]{1,0:T(8,128)(2,1)S(1)} %bitcast.184, s32[8,2]{1,0:T(8,128)S(1)} %copy.54.off), custom_call_target="tpu_custom_call" | custom-call | tf_op jit(solution)/shard_map/pallas_call | solution.py:616
  24.1 1.1 %convolution_bitcast_fusion.4 = bf16[8,4,12,32]{3,2,0,1:T(8,128)(2,1)S(1)} fusion(bf16[8,4,12,3,3]{2,3,4,0,1:T(4,128)(2,1)} %constant.61, bf16[32,3,3]{0,2,1:T(4,128)(2,1)} %bitcast.208), kind=kOutput, calls=%fused_computation.5 | convolution fusion | flops 221184 | bytes 32064 | tf_op jit(solution)/shard_map/arbyx,oyx->arbo/dot_general | solution.py:51
  25.6 0.7 bitcast_dynamic-update-slice_fusion.14
  27.7 0.7 bitcast_dynamic-update-slice_fusion.11
  28.4 0.7 bitcast_dynamic-update-slice_fusion.10
  30.0 0.7 bitcast_dynamic-update-slice_fusion.8
  30.7 0.7 bitcast_dynamic-update-slice_fusion.7
  31.4 0.7 bitcast_dynamic-update-slice_fusion.6
  32.8 0.7 bitcast_dynamic-update-slice_fusion.4
  33.5 0.7 bitcast_dynamic-update-slice_fusion.3
  34.2 0.7 bitcast_dynamic-update-slice_fusion.2
  34.9 0.7 bitcast_dynamic-update-slice_fusion.1
  35.6 0.7 bitcast_dynamic-update-slice_fusion.refs_1_
  37.0 1.0 reshape.97
  38.0 0.9 copy.100.refs_2_
  39.4 0.7 reshape.67.refs_3_
  40.5 2.1 %convolution_bitcast_fusion = bf16[3,16,64,4,64]{4,1,2,0,3:T(8,128)(2,1)S(1)} fusion(bf16[16,4,3,3,1,1]{0,2,3,5,4,1:T(4,128)(2,1)S(1)} %copy-done.24, bf16[3,3,3,64,64]{4,3,2,1,0:T(8,128)(2,1)S(1)} %reshape.68), kind=kOutput, calls=%fused_computation.1 | convolution fusion | flops 14155776 | bytes 1795200 | tf_op jit(solution)/shard_map/abyx,zyxco->zacbo/dot_general | solution.py:60
  42.6 2.4 %copy.76 = bf16[3,16,64,4,64]{4,3,2,1,0:T(4,128)(2,1)S(1)} copy(bf16[3,16,64,4,64]{4,1,2,0,3:T(8,128)(2,1)S(1)} %convolution_bitcast_fusion) | data formatting | bytes 3145728 | tf_op jit(solution)/shard_map/abyx,zyxco->zacbo/transpose | solution.py:60
  45.1 3.0 %reshape.69.refs_4_ = bf16[3,1024,256]{2,1,0:T(8,128)(2,1)} reshape(bf16[3,16,64,4,64]{4,3,2,1,0:T(4,128)(2,1)S(1)} %copy.76) | data formatting | bytes 3145728 | tf_op jit(solution)/shard_map/reshape | solution.py:60
  48.9 2.8 %reshape.98 = bf16[3,3,3,128,128]{4,3,2,1,0:T(8,128)(2,1)S(1)} reshape(bf16[3,3,3,16384]{3,2,1,0:T(4,128)(2,1)} %param.45) | data formatting | bytes 1769472 | tf_op jit(solution)/shard_map/reshape | solution.py:61
  52.3 2.4 %copy.79 = bf16[3,4,3,128,2,128]{5,4,3,2,1,0:T(2,128)(2,1)S(1)} copy(bf16[3,4,3,128,2,128]{5,3,2,0,4,1:T(8,128)(2,1)S(1)} %pad_maximum_fusion) | data formatting | bytes 4718592 | tf_op jit(solution)/shard_map/stack | solution.py:63
  54.8 2.8 %reshape.73.refs_6_ = bf16[3,1536,256]{2,1,0:T(8,128)(2,1)} reshape(bf16[3,4,3,128,2,128]{5,4,3,2,1,0:T(2,128)(2,1)S(1)} %copy.79) | data formatting | bytes 4718592 | tf_op jit(solution)/shard_map/reshape | solution.py:63
  57.8 0.8 copy.86.refs_7_
  59.1 0.7 reshape.99
  59.8 1.0 copy.102.refs_8_
  61.5 0.7 copy.87.refs_9_
  62.9 1.0 reshape.100
  63.9 1.0 copy.103.refs_10_
  71.3 31.8 %shard_map.308 = f32[3,8,8,128]{3,2,1,0:T(8,128)} custom-call(bf16[12,48,128]{2,1,0:T(8,128)(2,1)} %copy-done.1, bf16[15,256,384]{2,1,0:T(8,128)(2,1)} %bitcast_dynamic-update-slice_fusion.refs_1_, bf16[768,256]{1,0:T(8,128)(2,1)} %copy.100.refs_2_, bf16[256,128]{1,0:T(8,128)(2,1)} %reshape.67.refs_3_, bf16[3,1024,256]{2,1,0:T(8,128)(2,1)} %reshape.69.refs_4_, ...), custom_call_target="tpu_custom_call" | custom-call | tf_op jit(solution)/shard_map/pallas_call | solution.py:384
  103.0 1.6 %add_divide_fusion = f32[3,8,8,128]{3,2,1,0:T(8,128)} fusion(f32[3,8,8,128]{3,2,1,0:T(8,128)} %shard_map.308, f32[3]{0:T(128)S(1)} %copy-done.8), kind=kLoop, calls=%fused_computation.40 | loop fusion | flops 98304 | bytes 196620 | tf_op jit(solution)/shard_map/div | solution.py:645
  (96 shorter events, 15.2 us)
Async XLA Ops:
  0.0 48.1 %copy-start = (bf16[128,64,1,2,2]{0,4,3,2,1:T(2,128)(2,1)S(1)}, bf16[128,64,1,2,2]{0,4,3,2,1:T(2,128)(2,1)}, u32[]{:S(2)}) copy-start(bf16[128,64,1,2,2]{0,4,3,2,1:T(2,128)(2,1)} %param.43) | copy-start | bytes 196612
  0.8 0.7 copy-start.2
  23.4 0.7 copy-start.1
  29.1 7.2 %copy-start.17 = (bf16[32,32,1,3,3]{1,0,4,3,2:T(8,128)(2,1)S(1)}, bf16[32,32,1,3,3]{1,0,4,3,2:T(8,128)(2,1)}, u32[]{:S(2)}) copy-start(bf16[32,32,1,3,3]{1,0,4,3,2:T(8,128)(2,1)} %param.37) | copy-start | bytes 55300
  29.1 7.2 %copy-start.22 = (bf16[24,8,3,3,1]{0,2,3,4,1:T(4,128)(2,1)S(1)}, bf16[24,8,3,3,1]{0,2,3,4,1:T(4,128)(2,1)}, u32[]{:S(2)}) copy-start(bf16[24,8,3,3,1]{0,2,3,4,1:T(4,128)(2,1)} %constant.62) | copy-start | bytes 10372
  36.3 2.6 %copy-start.4 = (bf16[64,32,1,2,2]{0,4,3,2,1:T(2,128)(2,1)S(1)}, bf16[64,32,1,2,2]{0,4,3,2,1:T(2,128)(2,1)}, u32[]{:S(2)}) copy-start(bf16[64,32,1,2,2]{0,4,3,2,1:T(2,128)(2,1)} %param.39) | copy-start | bytes 49156
  36.3 2.6 %copy-start.6 = (bf16[4,2,2,1,1]{0,2,4,3,1:T(2,128)(2,1)S(1)}, bf16[4,2,2,1,1]{0,2,4,3,1:T(2,128)(2,1)}, u32[]{:S(2)}) copy-start(bf16[4,2,2,1,1]{0,2,4,3,1:T(2,128)(2,1)} %constant.63) | copy-start | bytes 100
  36.3 3.8 %copy-start.3 = (bf16[3,3,3,4096]{3,2,1,0:T(4,128)(2,1)S(1)}, bf16[3,3,3,4096]{3,2,1,0:T(4,128)(2,1)}, u32[]{:S(2)}) copy-start(bf16[3,3,3,4096]{3,2,1,0:T(4,128)(2,1)} %param.41) | copy-start | bytes 663556
  36.3 4.2 %copy-start.24 = (bf16[16,4,3,3,1,1]{0,2,3,5,4,1:T(4,128)(2,1)S(1)}, bf16[16,4,3,3,1,1]{0,2,3,5,4,1:T(4,128)(2,1)}, u32[]{:S(2)}) copy-start(bf16[16,4,3,3,1,1]{0,2,3,5,4,1:T(4,128)(2,1)} %constant.64) | copy-start | bytes 3460
  45.1 3.0 %copy-start.25 = (bf16[2,2,1,1]{1,0,3,2:T(2,128)(2,1)S(1)}, bf16[2,2,1,1]{1,0,3,2:T(2,128)(2,1)}, u32[]{:S(2)}) copy-start(bf16[2,2,1,1]{1,0,3,2:T(2,128)(2,1)} %constant.65) | copy-start | bytes 28
  54.8 2.8 %copy-start.19 = (bf16[128,64,1,2,2]{0,4,3,2,1:T(2,128)(2,1)S(1)}, bf16[128,64,1,2,2]{0,4,3,2,1:T(2,128)(2,1)}, u32[]{:S(2)}) copy-start(bf16[128,64,1,2,2]{0,4,3,2,1:T(2,128)(2,1)} %param.47) | copy-start | bytes 196612
  54.8 3.8 %copy-start.16 = (bf16[64,64,1,3,3]{1,0,4,3,2:T(8,128)(2,1)S(1)}, bf16[64,64,1,3,3]{1,0,4,3,2:T(8,128)(2,1)}, u32[]{:S(2)}) copy-start(bf16[64,64,1,3,3]{1,0,4,3,2:T(8,128)(2,1)} %param.49) | copy-start | bytes 221188
  54.8 3.8 %copy-start.23 = (bf16[16,4,3,3,1]{0,2,3,4,1:T(4,128)(2,1)S(1)}, bf16[16,4,3,3,1]{0,2,3,4,1:T(4,128)(2,1)}, u32[]{:S(2)}) copy-start(bf16[16,4,3,3,1]{0,2,3,4,1:T(4,128)(2,1)} %constant.66) | copy-start | bytes 3460
  57.6 3.2 %copy-start.5 = (bf16[64,32,1,2,2]{0,4,3,2,1:T(2,128)(2,1)S(1)}, bf16[64,32,1,2,2]{0,4,3,2,1:T(2,128)(2,1)}, u32[]{:S(2)}) copy-start(bf16[64,32,1,2,2]{0,4,3,2,1:T(2,128)(2,1)} %param.51) | copy-start | bytes 49156
  57.6 4.6 %copy-start.18 = (bf16[32,32,1,3,3]{1,0,4,3,2:T(8,128)(2,1)S(1)}, bf16[32,32,1,3,3]{1,0,4,3,2:T(8,128)(2,1)}, u32[]{:S(2)}) copy-start(bf16[32,32,1,3,3]{1,0,4,3,2:T(8,128)(2,1)} %param.53) | copy-start | bytes 55300
  61.4 3.5 %copy-start.7 = (bf16[3,32]{1,0:T(4,128)(2,1)S(1)}, bf16[3,32]{1,0:T(4,128)(2,1)}, u32[]{:S(2)}) copy-start(bf16[3,32]{1,0:T(4,128)(2,1)} %param.55) | copy-start | bytes 580
  61.4 4.3 %copy-start.9 = (f32[32]{0:T(128)S(1)}, f32[32]{0:T(128)}, u32[]{:S(2)}) copy-start(f32[32]{0:T(128)} %param.36) | copy-start | bytes 388
  61.4 4.9 %copy-start.10 = (f32[32]{0:T(128)S(1)}, f32[32]{0:T(128)}, u32[]{:S(2)}) copy-start(f32[32]{0:T(128)} %param.38) | copy-start | bytes 388
  61.4 5.6 %copy-start.20 = (f32[64]{0:T(128)S(1)}, f32[64]{0:T(128)}, u32[]{:S(2)}) copy-start(f32[64]{0:T(128)} %param.40) | copy-start | bytes 772
  61.4 6.1 %copy-start.11 = (f32[64]{0:T(128)S(1)}, f32[64]{0:T(128)}, u32[]{:S(2)}) copy-start(f32[64]{0:T(128)} %param.42) | copy-start | bytes 772
  61.4 6.8 %copy-start.21 = (f32[128]{0:T(128)S(1)}, f32[128]{0:T(128)}, u32[]{:S(2)}) copy-start(f32[128]{0:T(128)} %param.46) | copy-start | bytes 1540
  61.4 7.3 %copy-start.12 = (f32[64]{0:T(128)S(1)}, f32[64]{0:T(128)}, u32[]{:S(2)}) copy-start(f32[64]{0:T(128)} %param.48) | copy-start | bytes 772
  61.4 7.9 %copy-start.13 = (f32[64]{0:T(128)S(1)}, f32[64]{0:T(128)}, u32[]{:S(2)}) copy-start(f32[64]{0:T(128)} %param.50) | copy-start | bytes 772
  61.5 8.5 %copy-start.14 = (f32[32]{0:T(128)S(1)}, f32[32]{0:T(128)}, u32[]{:S(2)}) copy-start(f32[32]{0:T(128)} %param.52) | copy-start | bytes 388
  62.2 8.5 %copy-start.15 = (f32[32]{0:T(128)S(1)}, f32[32]{0:T(128)}, u32[]{:S(2)}) copy-start(f32[32]{0:T(128)} %param.54) | copy-start | bytes 388
  71.3 31.8 %copy-start.8 = (f32[3]{0:T(128)S(1)}, f32[3]{0:T(128)}, u32[]{:S(2)}) copy-start(f32[3]{0:T(128)} %param.56) | copy-start | bytes 40
where the time goes:
time: 105 us
  Pallas kernels  53.7 us (51%)
  local copies, waits for them, and re-layouts  42.4 us (40%)
  matrix products  6.05 us (6%)
  other arithmetic  2.18 us (2%)
    pallas_call x1, Pallas kernels, unet_call(): pl.pallas_call(body, out_shape=jax.ShapeDtypeStruct((3, 8, 8, 128), F32),...  31.8 us
    pallas_call x1, Pallas kernels, gather_call(): pl.pallas_call(body, out_shape=jax.ShapeDtypeStruct((NZ, 48, 128), BF), i...  21.9 us
    unnamed x67, local copies, waits for them, and re-layouts  11.3 us
    reshape x6, local copies, waits for them, and re-layouts, prep_weights(): d[name] = m.reshape(t.shape[0] * ch, 256)  5.61 us
    reshape x1, local copies, waits for them, and re-layouts, prep_weights(): jnp.einsum('abyx,zyxco->zacbo', t, kin).astype(BF).reshape(3, 1024, 256)  2.99 us
    reshape x1, local copies, waits for them, and re-layouts, prep_weights(): kb = w['bottom_kernel'].reshape(3, 3, 3, 128, 128)  2.8 us
    reshape x1, local copies, waits for them, and re-layouts, prep_weights(): jnp.stack([jnp.stack(q, 3) for q in rows], 1).reshape(3, 1536, 256)  2.79 us
    another operation x1, local copies, waits for them, and re-layouts, prep_weights(): jnp.stack([jnp.stack(q, 3) for q in rows], 1).reshape(3, 1536, 256)  2.45 us

commit v1 on v0

--- a/solution.py
+++ b/solution.py
@@ -1,5 +1,3 @@
-import functools
-import numpy as np
 import jax
 import jax.numpy as jnp
 from jax import lax
@@ -13,91 +11,6 @@
 NZ = 12
 R12, R10, R8 = NZ * PITCH, 10 * PITCH, 8 * PITCH
 PAD = 16
-
-
-def stem_table():
-    cols = [0, 1, 2, 3, 4, 5, -2, -1]
-    outs = [(ro, j) for ro in range(2) for j in range(4)] + [(0, 4), (1, -1), (1, 4), (0, -1)]
-    t = np.zeros((8, 4, 12, 3, 3), np.float32)
-    for a, i in enumerate(cols):
-        for r in range(4):
-            for b, (ro, j) in enumerate(outs):
-                dy, dx = r - ro, i - j + 1
-                if 0 <= dy < 3 and 0 <= dx < 3:
-                    t[a, r, b, dy, dx] = 1
-    return t
-
-
-def plane_table(width):
-    ks = [(r, i) for r in range(4) for i in range(width)]
-    if width == 4:
-        for h in range(2):
-            ks += [(2 * h, 4), (2 * h + 1, -1), (2 * h + 1, 4), (2 * h, -1)]
-    else:
-        for r in range(4):
-            ks += [(r, 2), (r, -1)]
-    outs = [(ro, j) for ro in range(2) for j in range(width)]
-    t = np.zeros((len(ks), len(outs), 3, 3), np.float32)
-    for a, (r, i) in enumerate(ks):
-        for b, (ro, j) in enumerate(outs):
-            dy, dx = r - ro, i - j + 1
-            if 0 <= dy < 3 and 0 <= dx < 3:
-                t[a, b, dy, dx] = 1
-    return t
-
-
-def prep_weights(w):
-    d = {}
-    base = jnp.einsum("arbyx,oyx->arbo", jnp.asarray(stem_table(), BF), w["stem_kernel"][:, 0, 0]).astype(BF)
-    base = base.reshape(8, 4, 384)
-    d["stem"] = jnp.stack([jnp.pad(base, ((0, 0), (2 * q, 28 - 2 * q), (0, 0))).reshape(256, 384) for q in range(15)])
-    for name, width, ch in (("outer", 4, 32), ("finish", 4, 32), ("mend", 2, 64)):
-        t = jnp.asarray(plane_table(width), BF)
-        m = jnp.einsum("abyx,ocyx->acbo", t, w[name + "_kernel"][:, :, 0]).astype(BF)
-        d[name] = m.reshape(t.shape[0] * ch, 256)
-    t = jnp.asarray(plane_table(2), BF)
-    kin = w["inner_kernel"].reshape(3, 3, 3, 64, 64)
-    d["inner"] = jnp.einsum("abyx,zyxco->zacbo", t, kin).astype(BF).reshape(3, 1024, 256)
-    kb = w["bottom_kernel"].reshape(3, 3, 3, 128, 128)
-    rows = [[kb[:, r - ro] if 0 <= r - ro < 3 else jnp.zeros_like(kb[:, 0]) for ro in range(2)] for r in range(4)]
-    d["bottom"] = jnp.stack([jnp.stack(q, 3) for q in rows], 1).reshape(3, 1536, 256)
-
-    def down(k, width):
-        eye = np.zeros((width, width // 2, 2), np.float32)
-        for i in range(width):
-            eye[i, i // 2, i % 2] = 1
-        m = jnp.einsum("ijq,ocpq->picjo", jnp.asarray(eye, BF), k[:, :, 0]).astype(BF)
-        return m.reshape(2 * width * k.shape[1], -1)
-
-    def up(k, width):
-        eye = np.zeros((width, width // 2, 2), np.float32)
-        for i in range(width):
-            eye[i, i // 2, i % 2] = 1
-        m = jnp.einsum("ijq,copq->jcpio", jnp.asarray(eye, BF), k[:, :, 0]).astype(BF)
-        return m.reshape(width // 2 * k.shape[0], -1)
-
-    d["pool"] = down(w["pooling_kernel"], 4)
-    d["narrow"] = down(w["narrowing_kernel"], 2)
-    d["lift"] = up(w["lift_kernel"], 2)
-    d["expand"] = up(w["expand_kernel"], 4)
-    hk = w["head_kernel"]
-    eye2 = jnp.eye(2, dtype=BF)
-    h = jnp.einsum("rs,oc->roscj", eye2, hk)[:, :, :, None, :, 0] if False else None
-    head = jnp.einsum("rs,j,oc->rosjc", eye2, jnp.ones((4,), BF), hk).astype(BF).reshape(6, 256)
-    d["head"] = jnp.pad(head, ((0, 2), (0, 0)))
-    b = {}
-    s4 = jnp.tile(w["stem_bias"], 12)
-    b["stem"] = s4[None]
-    b["outer"] = jnp.tile(w["outer_bias"], 8)[None]
-    b["finish"] = jnp.tile(w["finish_bias"], 8)[None]
-    b["expand"] = jnp.tile(w["expand_bias"], 8)[None]
-    b["pool"] = jnp.tile(w["pooling_bias"], 2)[None]
-    b["inner"] = jnp.tile(w["inner_bias"], 4)[None]
-    b["mend"] = jnp.tile(w["mend_bias"], 4)[None]
-    b["lift"] = jnp.tile(w["lift_bias"], 4)[None]
-    b["narrow"] = w["narrowing_bias"][None]
-    b["bottom"] = jnp.tile(w["bottom_bias"], 2)[None]
-    return d, b
 
 
 WN = ("stem", "outer", "pool", "inner", "narrow", "bottom", "lift", "mend", "expand", "finish", "head")
@@ -175,7 +88,10 @@
         res = jnp.concatenate([sc.s[2 * p + 1], sc.s[2 * p + 2]], axis=1).astype(F32)
         o = (acc + res + B["outer"][...]).astype(BF)
 
-        sc.o[p] = o[80:400]
+        @pl.when(jnp.logical_and(p >= 4, p < 10))
+        def _():
+            sc.o[p - 4] = o[80:400]
+
         pooled = (dot(o, W["pool"][...]) + B["pool"][...]).astype(BF).astype(F32)
         v = rowok(gy * 4 + p - 5, ngy * 4)
         pooled = pooled * sc.mask[v]
@@ -270,7 +186,7 @@
         for h in range(2):
             j = 2 * n + h
             up = dot(a[:, h * 128 : (h + 1) * 128], W["expand"][...])
-            x = (up + sc.o[4 + j].astype(F32) + B["expand"][...]).astype(BF).astype(F32)
+            x = (up + sc.o[j].astype(F32) + B["expand"][...]).astype(BF).astype(F32)
             for e in range(2):
                 t = 2 * j + e
                 v = rowok(gy * 8 + t - 2, ngy * 8)
@@ -296,19 +212,6 @@
     jl = (lane2 // 32) % 4
 
     def finish(u, _):
-        lhs = jnp.concatenate(
-            [sc.ea[2 * u + 1 + r] for r in range(4)] + [sc.ee[u], sc.ee[u + 1]], axis=1
-        )
-        acc = dot(lhs, W["finish"][...])
-        res = jnp.concatenate(
-            [sc.ef[2 * u + 2, PAD : PAD + R8], sc.ef[2 * u + 3, PAD : PAD + R8]], axis=1
-        )
-        f = (acc + res + B["finish"][...]).astype(BF).astype(F32)
-        sc.f[0:R8, 0] = f[:, 0:128]
-        sc.f[0:R8, 1] = f[:, 128:256]
-        return 0
-
-    def finish2(u, _):
         lhs = jnp.concatenate(
             [sc.ea[2 * u + 1 + r] for r in range(4)] + [sc.ee[u], sc.ee[u + 1]], axis=1
         )
@@ -332,7 +235,7 @@
                     out[o, z, pl.ds(2 * u + ro, 1), :] = lt[ro * 3 + o : ro * 3 + o + 1]
         return 0
 
-    lax.fori_loop(0, 4, finish2, 0)
+    lax.fori_loop(0, 4, finish, 0)
 
 
 SCRATCH = dict(
@@ -344,7 +247,7 @@
     s=((30, R12, 128), BF),
     r=((30, R12, 128), BF),
     e=((15, R12, 128), BF),
-    o=((14, R8, 256), BF),
+    o=((6, R8, 256), BF),
     pf=((14, R12 + 2 * PAD, 128), F32),
     pa=((14, R12, 256), BF),
     pb=((14, R12 + 16, 256), BF),
@@ -368,28 +271,248 @@
             setattr(self, n, r)
 
 
-def unet_call(pos_fn, counts, x4, d, b, interpret=False):
-    def body(*refs):
-        x4r = refs[0]
-        n = 1
-        W = dict(zip(WN, refs[n : n + len(WN)]))
-        n += len(WN)
-        B = dict(zip(BN, refs[n : n + len(BN)]))
-        n += len(BN)
-        out = refs[n]
-        sc = Refs(SCRATCH, refs[n + 1 :])
-        compute(pos_fn(), counts, x4r, W, B, out, sc)
-
-    vm = pl.BlockSpec(memory_space=pltpu.VMEM)
-    return pl.pallas_call(
-        body,
-        out_shape=jax.ShapeDtypeStruct((3, 8, 8, 128), F32),
-        in_specs=[vm] * (1 + len(WN) + len(BN)),
-        out_specs=vm,
-        scratch_shapes=[pltpu.VMEM(s, t) for s, t in SCRATCH.values()],
-        compiler_params=pltpu.CompilerParams(vmem_limit_bytes=60 * 1024 * 1024),
-        interpret=interpret,
-    )(x4, *[d[k] for k in WN], *[b[k] for k in BN])
+WS = dict(
+    stem=((15, 256, 384), BF),
+    outer=((768, 256), BF),
+    pool=((256, 128), BF),
+    inner=((3, 1024, 256), BF),
+    narrow=((256, 128), BF),
+    bottom=((3, 1536, 256), BF),
+    lift=((128, 256), BF),
+    mend=((1024, 256), BF),
+    expand=((128, 256), BF),
+    finish=((768, 256), BF),
+    head=((8, 256), BF),
+)
+BS = dict(
+    stem=(1, 384), outer=(1, 256), pool=(1, 128), inner=(1, 256), narrow=(1, 128), bottom=(1, 256),
+    lift=(1, 256), mend=(1, 256), expand=(1, 256), finish=(1, 256),
+)
+RAW = dict(
+    stem=(3, 3, 32), outer=(3, 3, 32, 32), pool=(32, 2, 2, 64), inner=(3, 3, 3, 4096), narrow=(64, 2, 2, 128),
+    bottom=(3, 3, 3, 16384), lift=(64, 2, 2, 128), mend=(3, 3, 64, 64), expand=(32, 2, 2, 64),
+    finish=(3, 3, 32, 32), head=(3, 32),
+)
+RAWB = dict(stem=32, outer=32, pool=64, inner=64, narrow=128, bottom=128, lift=64, mend=64, expand=32, finish=32)
+LONG = dict(
+    stem="stem", outer="outer", pool="pooling", inner="inner", narrow="narrowing", bottom="bottom", lift="lift",
+    mend="mend", expand="expand", finish="finish",
+)
+PS = dict(
+    st=((128 * 8, 128), F32),
+    sw=((288, 384), F32),
+    tb=((27, 128, 128), BF),
+)
+
+
+def raw_views(w):
+    def plane(k):
+        return k[:, :, 0].transpose(2, 3, 0, 1)
+
+    def inward(k):
+        return k[:, :, 0].transpose(1, 2, 3, 0)
+
+    raw = dict(
+        stem=w["stem_kernel"][:, 0, 0].transpose(1, 2, 0),
+        outer=plane(w["outer_kernel"]), mend=plane(w["mend_kernel"]), finish=plane(w["finish_kernel"]),
+        pool=inward(w["pooling_kernel"]), narrow=inward(w["narrowing_kernel"]),
+        lift=inward(w["lift_kernel"]), expand=inward(w["expand_kernel"]),
+        inner=w["inner_kernel"], bottom=w["bottom_kernel"], head=w["head_kernel"],
+    )
+    bias = {k: w[LONG[k] + "_bias"].reshape(1, -1) for k in RAWB}
+    return raw, bias
+
+
+def iota(shape, dim):
+    return lax.broadcasted_iota(jnp.int32, shape, dim)
+
+
+def onehot(cond):
+    return jnp.where(cond, 1.0, 0.0).astype(BF)
+
+
+def prep_bias(raw, B):
+    for k, n in RAWB.items():
+        v = raw[k][...]
+        reps = BS[k][1] // n
+        B[k][...] = v if reps == 1 else jnp.concatenate([v] * reps, axis=1)
+
+
+def prep_stem(raw, W, ps):
+    k = jnp.concatenate([raw["stem"][dy].astype(F32) for dy in range(3)] + [jnp.zeros((7, 32), F32)], axis=0)
+    e = onehot(iota((32, 384), 0) == iota((32, 384), 1) % 32)
+    kt = dot(k.astype(BF), e)
+    row, lane = iota((32, 384), 0), iota((32, 384), 1)
+    a, r, slot = row // 4, row % 4, lane // 32
+    i = jnp.where(a < 6, a, a - 8)
+    edge = slot >= 8
+    ro = jnp.where(edge, jnp.where(jnp.logical_or(slot == 8, slot == 11), 0, 1), slot // 4)
+    j = jnp.where(edge, jnp.where(slot % 2 == 0, 4, -1), slot % 4)
+    dy, dx = r - ro, i - j + 1
+    ok = jnp.logical_and(jnp.logical_and(dy >= 0, dy < 3), jnp.logical_and(dx >= 0, dx < 3))
+    idx = jnp.where(ok, 3 * dy + dx, -1)
+    base = jnp.zeros((32, 384), F32)
+    for d in range(9):
+        base = jnp.where(idx == d, kt[d : d + 1], base)
+    ps.sw[...] = jnp.zeros((288, 384), F32)
+    for a in range(8):
+        ps.sw[32 + a * 32 : 36 + a * 32] = base[4 * a : 4 * a + 4]
+    for q in range(15):
+        W["stem"][q] = ps.sw[32 - 2 * q : 288 - 2 * q].astype(BF)
+
+
+def prep_plane(k, W, ch, ps):
+
+    flat = jnp.concatenate([k[dy, dx] for dy in range(3) for dx in range(3)], axis=0)
+    e = onehot(iota((128, ch), 0) % ch == iota((128, ch), 1))
+    t = lax.dot_general(e, flat, (((1,), (1,)), ((), ())), preferred_element_type=F32).astype(BF)
+    n = 9 * ch
+    er, el = iota((n, 1152), 0), iota((n, 1152), 1)
+    spread = onehot(jnp.logical_and(er // ch == el // 128, er % ch == el % ch))
+    t = dot(t, spread).astype(BF)
+    blocks = [[t[:, (3 * dy + dx) * 128 : (3 * dy + dx + 1) * 128] for dx in range(3)] for dy in range(3)]
+    place_plane(blocks, W, ch)
+
+
+def place_plane(blocks, W, ch, base=None):
+    width = 128 // ch
+    row, lane = iota((128, 128), 0), iota((128, 128), 1)
+    i, j = row // ch, lane // ch
+    zero = jnp.zeros((128, 128), F32)
+    b32 = [[b.astype(F32) for b in q] for q in blocks]
+    diag = []
+    for dy in range(3):
+        m = zero
+        for dx in range(3):
+            m = jnp.where(i - j + 1 == dx, b32[dy][dx], m)
+        diag.append(m.astype(BF))
+    zb = zero.astype(BF)
+
+    def put(at, ro, v):
+        if base is None:
+            W[at : at + 128, ro * 128 : (ro + 1) * 128] = v
+        else:
+            W[base, at : at + 128, ro * 128 : (ro + 1) * 128] = v
+
+    for r in range(4):
+        for ro in range(2):
+            put(r * 128, ro, diag[r - ro] if 0 <= r - ro < 3 else zb)
+
+    def side(dy, dx):
+        if not 0 <= dy < 3:
+            return zero
+        return jnp.where(j == (width - 1 if dx == 2 else 0), b32[dy][dx], 0.0)
+
+    if ch == 32:
+        for h in range(2):
+            for ro in range(2):
+                a, b = 2 * h - ro, 2 * h + 1 - ro
+                v = jnp.where(i == 0, side(a, 2), jnp.where(i == 1, side(b, 0), jnp.where(i == 2, side(b, 2), side(a, 0))))
+                put(512 + h * 128, ro, v.astype(BF))
+    else:
+        for r in range(4):
+            for ro in range(2):
+                v = jnp.where(i == 0, side(r - ro, 2), side(r - ro, 0))
+                put(512 + r * 128, ro, v.astype(BF))
+
+
+def prep_inner(k, W, ps):
+    s = onehot(
+        jnp.logical_and(iota((128, 256), 0) // 64 == iota((128, 256), 1) // 128,
+                        iota((128, 256), 0) % 64 == iota((128, 256), 1) % 64)
+    )
+    ra, rl = iota((128, 64), 0), iota((128, 64), 1)
+    a = onehot((ra % 64) == 2 * (rl % 32) + rl // 32)
+
+    def plane(zy, _):
+        dz = zy // 3
+        dy = zy - 3 * dz
+        for p in range(32):
+            ps.st[p * 8 : p * 8 + 3] = k[dz, dy, :, p * 128 : (p + 1) * 128].astype(F32)
+        for dx in range(3):
+            m = dot(ps.st[pl.ds(dx, 32, 8), :].astype(BF), s)
+            m = jnp.concatenate([m[:, 0:128], m[:, 128:256]], axis=0).astype(BF)
+            ps.tb[3 * zy + dx] = dot(a, m).astype(BF)
+        return 0
+
+    lax.fori_loop(0, 9, plane, 0)
+    for dz in range(3):
+        blocks = [[ps.tb[9 * dz + 3 * dy + dx] for dx in range(3)] for dy in range(3)]
+        place_plane(blocks, W, 64, base=dz)
+
+
+def prep_bottom(k, W, ps):
+    zb = jnp.zeros((384, 128), BF)
+    for dz in range(3):
+        W[dz, 0:384, 128:256] = zb
+        W[dz, 1152:1536, 0:128] = zb
+
+    def plane(zy, _):
+        dz = zy // 3
+        dy = zy - 3 * dz
+        for c in range(128):
+            ps.st[c * 8 : c * 8 + 3] = k[dz, dy, :, c * 128 : (c + 1) * 128].astype(F32)
+        for dx in range(3):
+            m = ps.st[pl.ds(dx, 128, 8), :].astype(BF)
+            W[dz, pl.ds(pl.multiple_of(dy * 384 + dx * 128, 128), 128), 0:128] = m
+            W[dz, pl.ds(pl.multiple_of(dy * 384 + 384 + dx * 128, 128), 128), 128:256] = m
+        return 0
+
+    lax.fori_loop(0, 9, plane, 0)
+
+
+def corners(k, ch, ps):
+    n = k.shape[3]
+    for c in range(ch):
+        for p in range(2):
+            v = k[c, p].astype(F32)
+            ps.st[(2 * c + p) * 8 : (2 * c + p) * 8 + 2, 0:n] = v
+    return [[ps.st[pl.ds(8 * p + q, ch, 16), :] for q in range(2)] for p in range(2)]
+
+
+def prep_corners(raw, W, ps):
+    lane = iota((32, 128), 1)
+    for name in ("pool", "expand"):
+        x = corners(raw[name], 32, ps)
+        rows = []
+        for p in range(2):
+            for i in range(4):
+                v = jnp.where(lane < 64, x[p][i % 2], 0.0)
+                rows.append(v if i < 2 else pltpu.roll(v, 64, 1))
+        z = jnp.concatenate(rows, axis=0)
+        if name == "pool":
+            W["pool"][...] = z.astype(BF)
+        else:
+            W["expand"][...] = jnp.concatenate([z[0:128].T, z[128:256].T], axis=1).astype(BF)
+    x = corners(raw["narrow"], 64, ps)
+    W["narrow"][...] = jnp.concatenate([x[p][q] for p in range(2) for q in range(2)], axis=0).astype(BF)
+    x = corners(raw["lift"], 64, ps)
+    z = [jnp.concatenate([x[p][0], x[p][1]], axis=0) for p in range(2)]
+    W["lift"][...] = jnp.concatenate([z[0].T, z[1].T], axis=1).astype(BF)
+
+
+def prep_head(raw, W):
+    h = raw["head"][...].astype(F32)
+    h = jnp.concatenate([h, h, jnp.zeros((2, 32), F32)], axis=0).astype(BF)
+    e = onehot(iota((32, 256), 0) == iota((32, 256), 1) % 32)
+    t = dot(h, e)
+    row, lane = iota((8, 256), 0), iota((8, 256), 1)
+    ro = jnp.where(row < 3, 0, 1)
+    W["head"][...] = jnp.where(jnp.logical_and(row < 6, ro == lane // 128), t, 0.0).astype(BF)
+
+
+def prep_all(raw, rawb, W, B, ps):
+    prep_bias(rawb, B)
+    prep_stem(raw, W, ps)
+    prep_plane(raw["outer"], W["outer"], 32, ps)
+    prep_corners(raw, W, ps)
+    prep_inner(raw["inner"], W["inner"], ps)
+    prep_bottom(raw["bottom"], W["bottom"], ps)
+    prep_plane(raw["mend"], W["mend"], 64, ps)
+    prep_plane(raw["finish"], W["finish"], 32, ps)
+    prep_head(raw, W)
+
+
 MESH = pl.DeviceIdType.MESH
 
 
@@ -397,7 +520,7 @@
     return lax.axis_index("sec"), lax.axis_index("gy"), lax.axis_index("gx")
 
 
-def align(own, left, right, off, has_left, has_right, cs):
+def align(own, left, right, has_left, has_right, cs):
     lane = lax.broadcasted_iota(jnp.int32, (1, 128), 1)
 
     def shifts(ref, first, ok):
@@ -459,6 +582,8 @@
 
 
 CS = dict(
+    img=((64, 128), BF),
+    off=((2, 8), jnp.int32),
     near=((80, 128), BF),
     rb=((2, 80, 128), BF),
     sbuf=((8, 48, 128), BF),
@@ -470,7 +595,7 @@
 )
 
 
-def gather(img, off, cs, sems, counts):
+def gather(img_copy, off_copy, cs, sems, counts, first):
     send1, recv1, send2, send3, recv2 = sems
     sec, gy, gx = axis_position()
     nsec, ngy, ngx = counts
@@ -510,13 +635,15 @@
     to_down = jnp.logical_and(gy >= 6, below)
     expect = 7 + jnp.where(has_left, 1, 0) + jnp.where(has_right, 1, 0) + jnp.where(jnp.logical_or(to_up, to_down), 8, 0)
 
-    cs.near[0:64] = img[...]
-    r16 = lax.broadcasted_iota(jnp.int32, (16, 128), 0)
-    info = jnp.zeros((16, 128), F32)
-    for i in range(8):
-        info = jnp.where(r16 == i, off[i, 0].astype(F32), info)
-        info = jnp.where(r16 == 8 + i, off[i, 1].astype(F32), info)
-    cs.near[64:80] = info.astype(BF)
+    img_copy.wait()
+    off_copy.wait()
+
+    cs.near[0:64] = cs.img[...]
+    sh = cs.off[...].astype(F32)
+    r16 = iota((16, 8), 0)
+    info = jnp.where(r16 < 8, sh[0:1], sh[1:2])
+    info = jnp.sum(jnp.where(r16 % 8 == iota((16, 8), 1), info, 0.0), axis=1, keepdims=True)
+    cs.near[64:80] = jnp.broadcast_to(info, (16, 128)).astype(BF)
 
     pl.semaphore_wait(barrier, expect)
 
@@ -534,6 +661,8 @@
     def _():
         near_copy(1, gx - 1).start()
 
+    first()
+
     @pl.when(has_left)
     def _():
         near_copy(0, gx - 1).wait_recv()
@@ -542,7 +671,7 @@
     def _():
         near_copy(1, gx + 1).wait_recv()
 
-    align(cs.near, cs.rb.at[0], cs.rb.at[1], off, has_left, has_right, cs)
+    align(cs.near, cs.rb.at[0], cs.rb.at[1], has_left, has_right, cs)
 
     def far(g, slot, s, sem):
         return pltpu.make_async_remote_copy(
@@ -604,26 +733,64 @@
     return finish, drain
 
 
-def gather_call(images, offsets, counts):
-    def body(img, off, out, *rest):
-        cs = Refs(CS, rest[: len(CS)])
-        finish, drain = gather(img, off, cs, rest[len(CS) :], counts)
+def fused_call(images, offsets, raw, rawb, counts):
+    nin = 2 + len(RAW) + len(RAWB)
+
+    def body(*refs):
+        ins, out, rest = refs[:nin], refs[nin], refs[nin + 1 :]
+
+        def take(names):
+            nonlocal rest
+            head, rest = rest[: len(names)], rest[len(names) :]
+            return head
+
+        cs = Refs(CS, take(CS))
+        sc = Refs(SCRATCH, take(SCRATCH))
+        ps = Refs(PS, take(PS))
+        W = dict(zip(WS, take(WS)))
+        B = dict(zip(BS, take(BS)))
+        R = dict(zip(RAW, take(RAW)))
+        RB = dict(zip(RAWB, take(RAWB)))
+        load = rest[0]
+        sems = rest[1:]
+        targets = [cs.img, cs.off] + list(R.values()) + list(RB.values())
+        copies = [pltpu.make_async_copy(s, t, load.at[n]) for n, (s, t) in enumerate(zip(ins, targets))]
+        for c in copies:
+            c.start()
+
+        def first():
+            for c in copies[2:]:
+                c.wait()
+            prep_bias(RB, B)
+            prep_stem(R, W, ps)
+            prep_plane(R["outer"], W["outer"], 32, ps)
+
+        finish, drain = gather(copies[0], copies[1], cs, sems, counts, first)
+        prep_corners(R, W, ps)
+        prep_inner(R["inner"], W["inner"], ps)
+        prep_bottom(R["bottom"], W["bottom"], ps)
+        prep_plane(R["mend"], W["mend"], 64, ps)
+        prep_plane(R["finish"], W["finish"], 32, ps)
+        prep_head(R, W)
         finish()
         drain()
-        out[...] = cs.rx[...]
+        compute(axis_position(), counts, cs.rx, W, B, out, sc)
 
     dma = pltpu.SemaphoreType.DMA
+    scratch = list(CS.values()) + list(SCRATCH.values()) + list(PS.values()) + list(WS.values())
+    scratch += [(s, F32) for s in BS.values()] + [(s, BF) for s in RAW.values()]
+    scratch += [((1, n), F32) for n in RAWB.values()]
     return pl.pallas_call(
         body,
-        out_shape=jax.ShapeDtypeStruct((NZ, 48, 128), BF),
-        in_specs=[pl.BlockSpec(memory_space=pltpu.VMEM), pl.BlockSpec(memory_space=pltpu.SMEM)],
+        out_shape=jax.ShapeDtypeStruct((3, 8, 8, 128), F32),
+        in_specs=[pl.BlockSpec(memory_space=pl.ANY)] * nin,
         out_specs=pl.BlockSpec(memory_space=pltpu.VMEM),
-        scratch_shapes=[pltpu.VMEM(s, t) for s, t in CS.values()]
-        + [dma((2,)), dma((2,)), dma((8,)), dma((8,)), dma((12,))],
+        scratch_shapes=[pltpu.VMEM(s, t) for s, t in scratch]
+        + [dma((nin,)), dma((2,)), dma((2,)), dma((8,)), dma((8,)), dma((12,))],
         compiler_params=pltpu.CompilerParams(
-            vmem_limit_bytes=24 * 1024 * 1024, collective_id=0, has_side_effects=True
+            vmem_limit_bytes=62 * 1024 * 1024, collective_id=0, has_side_effects=True
         ),
-    )(images, offsets)
+    )(images, offsets, *[raw[k] for k in RAW], *[rawb[k] for k in RAWB])
 
 
 NAMES = (
@@ -639,9 +806,9 @@
 
     def per_device(*args):
         w = dict(zip(NAMES, args))
-        x4 = gather_call(w["images"].reshape(64, 128), w["offsets"].reshape(8, 2), counts)
-        d, b = prep_weights(w)
-        logits = unet_call(axis_position, counts, x4, d, b)
+        raw, rawb = raw_views(w)
+        offsets = w["offsets"][0, :, :, 0].T
+        logits = fused_call(w["images"].reshape(64, 128), offsets, raw, rawb, counts)
         return jax.nn.sigmoid(logits + w["head_bias"][:, None, None, None])
 
     in_specs = (P(("sec", "gy"), None, "gx"), P(("sec", "gy"), None, None, "gx")) + (P(),) * 22

time: 105 us -> 54.3 us (0.52)
  local copies, waits for them, and re-layouts: 42.4 us -> 0.01 us
  matrix products: 6.05 us -> 0 us
  Pallas kernels: 53.7 us -> 52.4 us
    reshape x17 -> x0, local copies, waits for them, and re-layouts: 18 us -> none  [the longest x6 5.61 us: prep_weights(): d[name] = m.reshape(t.shape[0] * ch, 256)]
    unnamed x67 -> x2, local copies, waits for them, and re-layouts: 11.3 us -> 0.01 us
    another operation x20 -> x0, local copies, waits for them, and re-layouts: 8.81 us -> none  [the longest x1 2.45 us: prep_weights(): jnp.stack([jnp.stack(q, 3) for q in rows], 1).reshape(3, 1536, 256)]
    dot_general x9 -> x0, matrix products: 6.05 us -> none  [the longest x1 2.1 us: prep_weights(): jnp.einsum('abyx,zyxco->zacbo', t, kin).astype(BF).reshape(3, 1024, 256)]
    transpose x5 -> x0, local copies, waits for them, and re-layouts: 3.37 us -> none  [the longest x1 2.44 us: prep_weights(): jnp.einsum('abyx,zyxco->zacbo', t, kin).astype(BF).reshape(3, 1024, 256)]
    pallas_call x2 -> x1, Pallas kernels: 53.7 us -> 52.4 us  [fused_call(): pl.pallas_call(body, out_shape=jax.ShapeDtypeStruct((3, 8, 8, 128), F32),...]
where the time goes in v1:
time: 54.3 us; the launch traced here: 54.1 us
  Pallas kernels  52.4 us (97%)
  other arithmetic  1.64 us (3%)
    pallas_call x1, Pallas kernels, fused_call(): pl.pallas_call(body, out_shape=jax.ShapeDtypeStruct((3, 8, 8, 128), F32),...  52.4 us
    div x1, other arithmetic, per_device(): return jax.nn.sigmoid(logits + w['head_bias'][:, None, None, None])  1.64 us

profile of v1, /device:TPU:31, one launch (start us, length us, event | category | flops | bytes accessed | tf_op | source)
XLA Modules:
  0.0 54.1 jit_solution(10755456619362353049)
XLA Ops:
  0.0 0.0 copy-start
  0.0 52.4 %shard_map.226 = f32[3,8,8,128]{3,2,1,0:T(8,128)} custom-call(bf16[64,128]{1,0:T(8,128)(2,1)} %bitcast.45, s32[2,8]{1,0:T(2,128)} %bitcast.47, bf16[3,3,32]{2,1,0:T(4,128)(2,1)} %bitcast.46, bf16[3,3,32,32]{3,2,1,0:T(8,128)(2,1)} %bitcast.39, bf16[32,2,2,64]{3,2,1,0:T(2,128)(2,1)} %bitcast.43, bf16[3,3,3,4096]{3,2,1,0:T(4,128)(2,1)} %refs_5_.1, ...), custom_call_target="tpu_custom_call" | custom-call | tf_op jit(solution)/shard_map/pallas_call | solution.py:783
  52.4 0.0 copy-done
  52.4 1.6 %add_divide_fusion = f32[3,8,8,128]{3,2,1,0:T(8,128)} fusion(f32[3,8,8,128]{3,2,1,0:T(8,128)} %shard_map.226, f32[3]{0:T(128)S(1)} %copy-done), kind=kLoop, calls=%fused_computation | loop fusion | flops 98304 | bytes 196620 | tf_op jit(solution)/shard_map/div | solution.py:812
Async XLA Ops:
  0.0 52.4 %copy-start = (f32[3]{0:T(128)S(1)}, f32[3]{0:T(128)}, u32[]{:S(2)}) copy-start(f32[3]{0:T(128)} %param.47) | copy-start | bytes 40

commit v2 on v1

--- a/solution.py
+++ b/solution.py
@@ -9,6 +9,7 @@
 F32 = jnp.float32
 PITCH = 40
 NZ = 12
+OUTER_GROUP, INNER_GROUP = 14, 3
 R12, R10, R8 = NZ * PITCH, 10 * PITCH, 8 * PITCH
 PAD = 16
 
@@ -62,180 +63,174 @@
         lane < 64, sc.xf[PAD + 1 : PAD + 1 + R12], sc.xf[PAD - 1 : PAD - 1 + R12]
     ).astype(BF)
 
-    def stem(q, _):
+    zero_bf = jnp.zeros((), BF)
+
+    for q in range(15):
         acc = dot(sc.xin[...], W["stem"][q]) + B["stem"][...]
         s = acc.astype(BF)
         va = rowok(gy * 8 + 2 * q - 11, ngy * 8)
         vb = rowok(gy * 8 + 2 * q - 10, ngy * 8)
-        sc.s[2 * q] = s[:, 0:128]
-        sc.s[2 * q + 1] = s[:, 128:256]
-        r = jnp.maximum(s, jnp.zeros((), BF))
-        sc.r[2 * q] = r[:, 0:128] * sc.smask[va]
-        sc.r[2 * q + 1] = r[:, 128:256] * sc.smask[vb]
+        sc.se[q] = s[:, 0:128]
+        sc.so[q] = s[:, 128:256]
+        r = jnp.maximum(s, zero_bf)
+        sc.re[q] = r[:, 0:128] * sc.smask[va]
+        sc.ro[q] = r[:, 128:256] * sc.smask[vb]
         sc.e[q] = r[:, 256:384] * sc.emask[2 * va + vb]
-        return 0
-
-    lax.fori_loop(0, 15, stem, 0)
+
+    def flat(ref, start, count, *rest):
+        v = ref[(pl.ds(start, count),) + rest]
+        return v.reshape(count * v.shape[1], v.shape[2])
 
     sc.pf[:, 0:PAD] = jnp.zeros((14, PAD, 128), F32)
     sc.pf[:, PAD + R12 :] = jnp.zeros((14, PAD, 128), F32)
 
-    def outer(p, _):
+    NP = OUTER_GROUP
+
+    def outer(c, _):
+        p = c * NP
         lhs = jnp.concatenate(
-            [sc.r[2 * p], sc.r[2 * p + 1], sc.r[2 * p + 2], sc.r[2 * p + 3], sc.e[p], sc.e[p + 1]], axis=1
+            [flat(x, p + h, NP) for h in range(2) for x in (sc.re, sc.ro)] + [flat(sc.e, p, NP), flat(sc.e, p + 1, NP)],
+            axis=1,
         )
         acc = dot(lhs, W["outer"][...])
-        res = jnp.concatenate([sc.s[2 * p + 1], sc.s[2 * p + 2]], axis=1).astype(F32)
+        res = jnp.concatenate([flat(sc.so, p, NP), flat(sc.se, p + 1, NP)], axis=1).astype(F32)
         o = (acc + res + B["outer"][...]).astype(BF)
-
-        @pl.when(jnp.logical_and(p >= 4, p < 10))
-        def _():
-            sc.o[p - 4] = o[80:400]
-
+        for i in range(NP):
+            @pl.when(jnp.logical_and(p + i >= 4, p + i < 10))
+            def _():
+                sc.o[p + i - 4] = o[i * R12 + 80 : i * R12 + 400]
         pooled = (dot(o, W["pool"][...]) + B["pool"][...]).astype(BF).astype(F32)
-        v = rowok(gy * 4 + p - 5, ngy * 4)
-        pooled = pooled * sc.mask[v]
-        sc.pf[p, PAD : PAD + R12] = pooled
-        sc.pa[p, :, 0:128] = jnp.maximum(pooled, 0.0).astype(BF)
-        ea = jnp.where(lane < 64, sc.pf[p, PAD + 1 : PAD + 1 + R12], sc.pf[p, PAD - 1 : PAD - 1 + R12])
-        sc.pa[p, :, 128:256] = jnp.maximum(ea, 0.0).astype(BF)
-        sc.pb[p, :, 0:128] = jnp.maximum(sc.pf[p, PAD - 8 : PAD + 8 + R12], 0.0).astype(BF)
-        eb = jnp.where(lane < 64, sc.pf[p, PAD - 7 : PAD + 9 + R12], sc.pf[p, PAD - 9 : PAD + 7 + R12])
-        sc.pb[p, :, 128:256] = jnp.maximum(eb, 0.0).astype(BF)
+        for i in range(NP):
+            v = rowok(gy * 4 + p + i - 5, ngy * 4)
+            sc.pf[p + i, PAD : PAD + R12] = pooled[i * R12 : (i + 1) * R12] * sc.mask[v]
+        for i in range(NP):
+            q = p + i
+            relu = lambda v: jnp.maximum(v, 0.0).astype(BF)
+            sc.pa[q, :, 0:128] = relu(sc.pf[q, PAD : PAD + R12])
+            ea = jnp.where(lane < 64, sc.pf[q, PAD + 1 : PAD + 1 + R12], sc.pf[q, PAD - 1 : PAD - 1 + R12])
+            sc.pa[q, :, 128:256] = relu(ea)
+            sc.pb[q, :, 0:128] = relu(sc.pf[q, PAD - 8 : PAD + 8 + R12])
+            eb = jnp.where(lane < 64, sc.pf[q, PAD - 7 : PAD + 9 + R12], sc.pf[q, PAD - 9 : PAD + 7 + R12])
+            sc.pb[q, :, 128:256] = relu(eb)
         return 0
 
-    lax.fori_loop(0, 14, outer, 0)
+    lax.fori_loop(0, 14 // NP, outer, 0)
 
     sc.qf[:, 0:PAD] = jnp.zeros((6, PAD, 128), F32)
     sc.qf[:, PAD + R10 :] = jnp.zeros((6, PAD, 128), F32)
 
-    def inner(k, _):
-        acc = jnp.zeros((R10, 256), F32)
+    NK = INNER_GROUP
+
+    def rows4(get, count):
+        return [jnp.concatenate([get(2 * k + r) for k in range(count)], axis=0) for r in range(4)]
+
+    def inner(c, _):
+        k0 = c * NK
+        pieces = []
         for dz in range(3):
             src = (sc.pa, sc.pb, sc.pa)[dz]
             lo = (0, 48, 80)[dz]
-            lhs = jnp.concatenate(
-                [src[2 * k + r, lo : lo + R10, 0:128] for r in range(4)]
-                + [src[2 * k + r, lo : lo + R10, 128:256] for r in range(4)],
-                axis=1,
-            )
-            acc = acc + dot(lhs, W["inner"][dz])
+            for half in range(2):
+                pieces += rows4(
+                    lambda t: src[2 * k0 + t, lo : lo + R10, half * 128 : half * 128 + 128], NK
+                )
+        acc = dot(jnp.concatenate(pieces, axis=1), W["inner"][...].reshape(3072, 256))
         res = jnp.concatenate(
-            [sc.pf[2 * k + 1, PAD + 40 : PAD + 440], sc.pf[2 * k + 2, PAD + 40 : PAD + 440]], axis=1
+            [
+                jnp.concatenate([sc.pf[2 * (k0 + k) + 1 + h, PAD + 40 : PAD + 440] for k in range(NK)], axis=0)
+                for h in range(2)
+            ],
+            axis=1,
         )
         a = (acc + res + B["inner"][...]).astype(BF)
-        sc.i[k] = a.astype(F32)[40:360].astype(BF)
+        for k in range(NK):
+            sc.i[k0 + k] = a[k * R10 : (k + 1) * R10].astype(F32)[40:360].astype(BF)
         sq = (dot(a, W["narrow"][...]) + B["narrow"][...]).astype(BF).astype(F32)
-        v = rowok(gy * 2 + k - 2, ngy * 2)
-        sq = sq * sc.mask[v, 40:440]
-        sc.qf[k, PAD : PAD + R10] = sq
-        for d in range(3):
-            sc.qa[k, :, d * 128 : (d + 1) * 128] = jnp.maximum(
-                sc.qf[k, PAD - 1 + d : PAD - 1 + d + R10], 0.0
-            ).astype(BF)
-            sc.qb[k, :, d * 128 : (d + 1) * 128] = jnp.maximum(
-                sc.qf[k, PAD - 9 + d : PAD + 7 + d + R10], 0.0
-            ).astype(BF)
+        for k in range(NK):
+            v = rowok(gy * 2 + k0 + k - 2, ngy * 2)
+            sc.qf[k0 + k, PAD : PAD + R10] = sq[k * R10 : (k + 1) * R10] * sc.mask[v, 40:440]
+        for k in range(NK):
+            for d in range(3):
+                sc.qa[k0 + k, :, d * 128 : (d + 1) * 128] = jnp.maximum(
+                    sc.qf[k0 + k, PAD - 1 + d : PAD - 1 + d + R10], 0.0
+                ).astype(BF)
+                sc.qb[k0 + k, :, d * 128 : (d + 1) * 128] = jnp.maximum(
+                    sc.qf[k0 + k, PAD - 9 + d : PAD + 7 + d + R10], 0.0
+                ).astype(BF)
         return 0
 
-    lax.fori_loop(0, 6, inner, 0)
+    lax.fori_loop(0, 6 // NK, inner, 0)
 
     sc.lf[:, 0:PAD] = jnp.zeros((8, PAD, 128), F32)
     sc.lf[:, PAD + R8 :] = jnp.zeros((8, PAD, 128), F32)
 
-    def bottom(mi, _):
-        acc = jnp.zeros((R8, 256), F32)
-        for dz in range(3):
-            src = (sc.qa, sc.qb, sc.qa)[dz]
-            lo = (0, 48, 80)[dz]
-            lhs = jnp.concatenate([src[2 * mi + r, lo : lo + R8, :] for r in range(4)], axis=1)
-            acc = acc + dot(lhs, W["bottom"][dz])
-        res = jnp.concatenate(
-            [sc.qf[2 * mi + 1, PAD + 40 : PAD + 360], sc.qf[2 * mi + 2, PAD + 40 : PAD + 360]], axis=1
-        )
-        a = (acc + res + B["bottom"][...]).astype(BF)
-        for h in range(2):
-            up = dot(a[:, h * 128 : (h + 1) * 128], W["lift"][...])
-            y = 2 * mi + h
-            l = (up + sc.i[y + 1].astype(F32) + B["lift"][...]).astype(BF).astype(F32)
-            for e in range(2):
-                t = 2 * y + e
-                v = rowok(gy * 4 + t - 2, ngy * 4)
-                lm = l[:, e * 128 : (e + 1) * 128] * sc.mask[v, 80:400]
-                sc.lf[t, PAD : PAD + R8] = lm
-                sc.la[t, :, 0:128] = jnp.maximum(lm, 0.0).astype(BF)
-                ed = jnp.where(lane < 64, sc.lf[t, PAD + 1 : PAD + 1 + R8], sc.lf[t, PAD - 1 : PAD - 1 + R8])
-                sc.la[t, :, 128:256] = jnp.maximum(ed, 0.0).astype(BF)
-        return 0
-
-    lax.fori_loop(0, 2, bottom, 0)
-
-    sc.ef[:, 0:PAD] = jnp.zeros((12, PAD, 128), F32)
-    sc.ef[:, PAD + R8 :] = jnp.zeros((12, PAD, 128), F32)
-
-    def mend(n, _):
-        lhs = jnp.concatenate(
-            [sc.la[2 * n + r, :, 0:128] for r in range(4)] + [sc.la[2 * n + r, :, 128:256] for r in range(4)],
-            axis=1,
-        )
-        acc = dot(lhs, W["mend"][...])
-        res = jnp.concatenate(
-            [sc.lf[2 * n + 1, PAD : PAD + R8], sc.lf[2 * n + 2, PAD : PAD + R8]], axis=1
-        )
-        a = (acc + res + B["mend"][...]).astype(BF)
-        for h in range(2):
-            j = 2 * n + h
-            up = dot(a[:, h * 128 : (h + 1) * 128], W["expand"][...])
-            x = (up + sc.o[j].astype(F32) + B["expand"][...]).astype(BF).astype(F32)
-            for e in range(2):
-                t = 2 * j + e
-                v = rowok(gy * 8 + t - 2, ngy * 8)
-                xm = x[:, e * 128 : (e + 1) * 128] * sc.mask[v, 80:400]
-                sc.ef[t, PAD : PAD + R8] = xm
-                sc.ea[t] = jnp.maximum(xm, 0.0).astype(BF)
-        return 0
-
-    lax.fori_loop(0, 3, mend, 0)
-
-    def edges(u, _):
+    pieces = []
+    for dz in range(3):
+        src = (sc.qa, sc.qb, sc.qa)[dz]
+        lo = (0, 48, 80)[dz]
+        pieces += rows4(lambda t: src[t, lo : lo + R8, :], 2)
+    acc = dot(jnp.concatenate(pieces, axis=1), W["bottom"][...].reshape(4608, 256))
+    res = jnp.concatenate(
+        [jnp.concatenate([sc.qf[2 * k + 1 + h, PAD + 40 : PAD + 360] for k in range(2)], axis=0) for h in range(2)],
+        axis=1,
+    )
+    a = (acc + res + B["bottom"][...]).astype(BF)
+    a = jnp.concatenate([a[k * R8 : (k + 1) * R8, h * 128 : h * 128 + 128] for k in range(2) for h in range(2)], axis=0)
+    up = dot(a, W["lift"][...])
+    l = (up + flat(sc.i, 1, 4).astype(F32) + B["lift"][...]).astype(BF).astype(F32)
+    for t in range(8):
+        y, e = t // 2, t % 2
+        v = rowok(gy * 4 + t - 2, ngy * 4)
+        sc.lf[t, PAD : PAD + R8] = l[y * R8 : (y + 1) * R8, e * 128 : (e + 1) * 128] * sc.mask[v, 80:400]
+    for t in range(8):
+        sc.pa[t, 0:R8, 0:128] = jnp.maximum(sc.lf[t, PAD : PAD + R8], 0.0).astype(BF)
+        ed = jnp.where(lane < 64, sc.lf[t, PAD + 1 : PAD + 1 + R8], sc.lf[t, PAD - 1 : PAD - 1 + R8])
+        sc.pa[t, 0:R8, 128:256] = jnp.maximum(ed, 0.0).astype(BF)
+
+    pieces = rows4(lambda t: sc.pa[t, 0:R8, 0:128], 3) + rows4(lambda t: sc.pa[t, 0:R8, 128:256], 3)
+    acc = dot(jnp.concatenate(pieces, axis=1), W["mend"][...])
+    res = jnp.concatenate(
+        [jnp.concatenate([sc.lf[2 * k + 1 + h, PAD : PAD + R8] for k in range(3)], axis=0) for h in range(2)], axis=1
+    )
+    a = (acc + res + B["mend"][...]).astype(BF)
+    a = jnp.concatenate([a[k * R8 : (k + 1) * R8, h * 128 : h * 128 + 128] for k in range(3) for h in range(2)], axis=0)
+    up = dot(a, W["expand"][...])
+    x = (up + flat(sc.o, 0, 6).astype(F32) + B["expand"][...]).astype(BF).astype(F32)
+    for t in range(1, 11):
+        j, e = t // 2, t % 2
+        v = rowok(gy * 8 + t - 2, ngy * 8)
+        xm = x[j * R8 : (j + 1) * R8, e * 128 : (e + 1) * 128] * sc.mask[v, 80:400]
+        sc.pf[t, PAD : PAD + R8] = xm
+        sc.re[t, 0:R8] = jnp.maximum(xm, 0.0).astype(BF)
+    for u in range(5):
         ta, tb = 2 * u + 1, 2 * u + 2
-        ua = jnp.where(lane < 64, sc.ef[ta, PAD + 1 : PAD + 1 + R8], sc.ef[ta, PAD - 1 : PAD - 1 + R8])
-        ub = jnp.where(lane < 64, sc.ef[tb, PAD + 1 : PAD + 1 + R8], sc.ef[tb, PAD - 1 : PAD - 1 + R8])
+        ua = jnp.where(lane < 64, sc.pf[ta, PAD + 1 : PAD + 1 + R8], sc.pf[ta, PAD - 1 : PAD - 1 + R8])
+        ub = jnp.where(lane < 64, sc.pf[tb, PAD + 1 : PAD + 1 + R8], sc.pf[tb, PAD - 1 : PAD - 1 + R8])
         ub = pltpu.roll(ub, 64, 1)
         e = jnp.where(jnp.logical_and(lane >= 32, lane < 96), ub, ua)
-        sc.ee[u] = jnp.maximum(e, 0.0).astype(BF)
-        return 0
-
-    lax.fori_loop(0, 5, edges, 0)
-
-    lane2 = lax.broadcasted_iota(jnp.int32, (1, 256), 1)
-    jl = (lane2 // 32) % 4
-
-    def finish(u, _):
-        lhs = jnp.concatenate(
-            [sc.ea[2 * u + 1 + r] for r in range(4)] + [sc.ee[u], sc.ee[u + 1]], axis=1
-        )
-        acc = dot(lhs, W["finish"][...])
-        res = jnp.concatenate(
-            [sc.ef[2 * u + 2, PAD : PAD + R8], sc.ef[2 * u + 3, PAD : PAD + R8]], axis=1
-        )
-        f = (acc + res + B["finish"][...]).astype(BF).astype(F32)
-        for h in range(2):
-            sc.f[h, 0:R8] = f[:, h * 128 : (h + 1) * 128]
+        sc.e[u, 0:R8] = jnp.maximum(e, 0.0).astype(BF)
+
+    pieces = rows4(lambda t: sc.re[t + 1, 0:R8], 4) + [flat(sc.e, 0, 4, slice(0, R8)), flat(sc.e, 1, 4, slice(0, R8))]
+    acc = dot(jnp.concatenate(pieces, axis=1), W["finish"][...])
+    res = jnp.concatenate(
+        [jnp.concatenate([sc.pf[2 * k + 2 + h, PAD : PAD + R8] for k in range(4)], axis=0) for h in range(2)], axis=1
+    )
+    f = (acc + res + B["finish"][...]).astype(BF).astype(F32)
+    for h in range(2):
+        for u in range(4):
+            sc.f[h, u] = f[u * R8 : (u + 1) * R8, h * 128 : (h + 1) * 128]
+    for u in range(4):
         for h in range(2):
             for z in range(8):
-                fz = sc.f[h, z * PITCH + 3 : z * PITCH + 35]
+                fz = sc.f[h, u, z * PITCH + 3 : z * PITCH + 35]
                 for j in range(4):
-                    sc.g[h, pl.ds(z * 128 + j, 32, 4), :] = jnp.where(lane // 32 == j, fz, 0.0)
+                    sc.g[u % 2, h, pl.ds(z * 128 + j, 32, 4), :] = jnp.where(lane // 32 == j, fz, 0.0)
+        gz = jnp.concatenate([sc.g[u % 2, h] for h in range(2)], axis=1).astype(BF)
+        lt = lax.dot_general(W["head"][...], gz, (((1,), (1,)), ((), ())), preferred_element_type=F32)
         for z in range(8):
-            gz = jnp.concatenate([sc.g[h, z * 128 : (z + 1) * 128] for h in range(2)], axis=1).astype(BF)
-            lt = lax.dot_general(W["head"][...], gz, (((1,), (1,)), ((), ())), preferred_element_type=F32)
             for ro in range(2):
                 for o in range(3):
-                    out[o, z, pl.ds(2 * u + ro, 1), :] = lt[ro * 3 + o : ro * 3 + o + 1]
-        return 0
-
-    lax.fori_loop(0, 4, finish, 0)
+                    out[o, z, 2 * u + ro : 2 * u + ro + 1, :] = lt[ro * 3 + o : ro * 3 + o + 1, z * 128 : z * 128 + 128]
 
 
 SCRATCH = dict(
@@ -244,8 +239,10 @@
     emask=((4, R12, 128), BF),
     xf=((R12 + 2 * PAD, 128), F32),
     xin=((R12, 256), BF),
-    s=((30, R12, 128), BF),
-    r=((30, R12, 128), BF),
+    se=((15, R12, 128), BF),
+    so=((15, R12, 128), BF),
+    re=((15, R12, 128), BF),
+    ro=((15, R12, 128), BF),
     e=((15, R12, 128), BF),
     o=((6, R8, 256), BF),
     pf=((14, R12 + 2 * PAD, 128), F32),
@@ -256,12 +253,8 @@
     qa=((6, R10, 384), BF),
     qb=((6, R10 + 16, 384), BF),
     lf=((8, R8 + 2 * PAD, 128), F32),
-    la=((8, R8, 256), BF),
-    ef=((12, R8 + 2 * PAD, 128), F32),
-    ea=((12, R8, 128), BF),
-    ee=((5, R8, 128), BF),
-    f=((2, R8, 128), F32),
-    g=((2, 1024, 128), F32),
+    f=((2, 4, R8, 128), F32),
+    g=((2, 2, 1024, 128), F32),
 )
 
 

time: 54.3 us -> 44.3 us (0.82)
  Pallas kernels: 52.4 us -> 42.4 us
    pallas_call x1, Pallas kernels: 52.4 us -> 42.4 us  [fused_call(): pl.pallas_call(body, out_shape=jax.ShapeDtypeStruct((3, 8, 8, 128), F32),...]
where the time goes in v2:
time: 44.3 us; the launch traced here: 44.1 us
  Pallas kernels  42.4 us (96%)
  other arithmetic  1.64 us (4%)
    pallas_call x1, Pallas kernels, fused_call(): pl.pallas_call(body, out_shape=jax.ShapeDtypeStruct((3, 8, 8, 128), F32),...  42.4 us
    div x1, other arithmetic, per_device(): return jax.nn.sigmoid(logits + w['head_bias'][:, None, None, None])  1.64 us

profile of v2, /device:TPU:31, one launch (start us, length us, event | category | flops | bytes accessed | tf_op | source)
XLA Modules:
  0.0 44.1 jit_solution(13948946788794009429)
XLA Ops:
  0.0 0.0 copy-start
  0.0 42.4 %shard_map.226 = f32[3,8,8,128]{3,2,1,0:T(8,128)} custom-call(bf16[64,128]{1,0:T(8,128)(2,1)} %bitcast.45, s32[2,8]{1,0:T(2,128)} %bitcast.47, bf16[3,3,32]{2,1,0:T(4,128)(2,1)} %bitcast.46, bf16[3,3,32,32]{3,2,1,0:T(8,128)(2,1)} %bitcast.39, bf16[32,2,2,64]{3,2,1,0:T(2,128)(2,1)} %bitcast.43, bf16[3,3,3,4096]{3,2,1,0:T(4,128)(2,1)} %refs_5_.1, ...), custom_call_target="tpu_custom_call" | custom-call | tf_op jit(solution)/shard_map/pallas_call | solution.py:776
  42.4 0.0 copy-done
  42.4 1.6 %add_divide_fusion = f32[3,8,8,128]{3,2,1,0:T(8,128)} fusion(f32[3,8,8,128]{3,2,1,0:T(8,128)} %shard_map.226, f32[3]{0:T(128)S(1)} %copy-done), kind=kLoop, calls=%fused_computation | loop fusion | flops 98304 | bytes 196620 | tf_op jit(solution)/shard_map/div | solution.py:805
Async XLA Ops:
  0.0 42.4 %copy-start = (f32[3]{0:T(128)S(1)}, f32[3]{0:T(128)}, u32[]{:S(2)}) copy-start(f32[3]{0:T(128)} %param.47) | copy-start | bytes 40

commit v3 on v2

--- a/solution.py
+++ b/solution.py
@@ -294,7 +294,8 @@
 PS = dict(
     st=((128 * 8, 128), F32),
     sw=((288, 384), F32),
-    tb=((27, 128, 128), BF),
+    ma=((864, 128), BF),
+    mb=((864, 256), BF),
 )
 
 
@@ -417,20 +418,25 @@
     ra, rl = iota((128, 64), 0), iota((128, 64), 1)
     a = onehot((ra % 64) == 2 * (rl % 32) + rl // 32)
 
-    def plane(zy, _):
-        dz = zy // 3
-        dy = zy - 3 * dz
+    for zy in range(9):
+        dz, dy = zy // 3, zy % 3
+        at = (zy % 4) * 256
         for p in range(32):
-            ps.st[p * 8 : p * 8 + 3] = k[dz, dy, :, p * 128 : (p + 1) * 128].astype(F32)
+            ps.st[at + p * 8 : at + p * 8 + 3] = k[dz, dy, :, p * 128 : (p + 1) * 128].astype(F32)
         for dx in range(3):
-            m = dot(ps.st[pl.ds(dx, 32, 8), :].astype(BF), s)
-            m = jnp.concatenate([m[:, 0:128], m[:, 128:256]], axis=0).astype(BF)
-            ps.tb[3 * zy + dx] = dot(a, m).astype(BF)
-        return 0
-
-    lax.fori_loop(0, 9, plane, 0)
+            d = 3 * zy + dx
+            ps.ma[d * 32 : d * 32 + 32] = ps.st[pl.ds(at + dx, 32, 8), :].astype(BF)
+    ps.mb[...] = dot(ps.ma[...], s).astype(BF)
+    cols = [
+        jnp.concatenate([ps.mb[d * 32 : d * 32 + 32, 0:128], ps.mb[d * 32 : d * 32 + 32, 128:256]], axis=0)
+        for d in range(27)
+    ]
+    t = dot(a, jnp.concatenate(cols, axis=1)).astype(BF)
     for dz in range(3):
-        blocks = [[ps.tb[9 * dz + 3 * dy + dx] for dx in range(3)] for dy in range(3)]
+        blocks = [
+            [t[:, (9 * dz + 3 * dy + dx) * 128 : (9 * dz + 3 * dy + dx + 1) * 128] for dx in range(3)]
+            for dy in range(3)
+        ]
         place_plane(blocks, W, 64, base=dz)
 
 

time: 44.3 us -> 43.6 us (0.984)
  Pallas kernels: 42.4 us -> 41.7 us
    pallas_call x1, Pallas kernels: 42.4 us -> 41.7 us  [fused_call(): pl.pallas_call(body, out_shape=jax.ShapeDtypeStruct((3, 8, 8, 128), F32),...]
where the time goes in v3:
time: 43.6 us; the launch traced here: 43.4 us
  Pallas kernels  41.7 us (96%)
  other arithmetic  1.64 us (4%)
    pallas_call x1, Pallas kernels, fused_call(): pl.pallas_call(body, out_shape=jax.ShapeDtypeStruct((3, 8, 8, 128), F32),...  41.7 us
    div x1, other arithmetic, per_device(): return jax.nn.sigmoid(logits + w['head_bias'][:, None, None, None])  1.64 us

profile of v3, /device:TPU:31, one launch (start us, length us, event | category | flops | bytes accessed | tf_op | source)
XLA Modules:
  0.0 43.4 jit_solution(14584915143720935052)
XLA Ops:
  0.0 0.0 copy-start
  0.0 41.7 %shard_map.226 = f32[3,8,8,128]{3,2,1,0:T(8,128)} custom-call(bf16[64,128]{1,0:T(8,128)(2,1)} %bitcast.45, s32[2,8]{1,0:T(2,128)} %bitcast.47, bf16[3,3,32]{2,1,0:T(4,128)(2,1)} %bitcast.46, bf16[3,3,32,32]{3,2,1,0:T(8,128)(2,1)} %bitcast.39, bf16[32,2,2,64]{3,2,1,0:T(2,128)(2,1)} %bitcast.43, bf16[3,3,3,4096]{3,2,1,0:T(4,128)(2,1)} %refs_5_.1, ...), custom_call_target="tpu_custom_call" | custom-call | tf_op jit(solution)/shard_map/pallas_call | solution.py:782
  41.7 0.0 copy-done
  41.7 1.6 %add_divide_fusion = f32[3,8,8,128]{3,2,1,0:T(8,128)} fusion(f32[3,8,8,128]{3,2,1,0:T(8,128)} %shard_map.226, f32[3]{0:T(128)S(1)} %copy-done), kind=kLoop, calls=%fused_computation | loop fusion | flops 98304 | bytes 196620 | tf_op jit(solution)/shard_map/div | solution.py:811
Async XLA Ops:
  0.0 41.7 %copy-start = (f32[3]{0:T(128)S(1)}, f32[3]{0:T(128)}, u32[]{:S(2)}) copy-start(f32[3]{0:T(128)} %param.47) | copy-start | bytes 40

commit v4 on v3

--- a/solution.py
+++ b/solution.py
@@ -22,7 +22,7 @@
     return jnp.dot(a, b, preferred_element_type=F32)
 
 
-def compute(pos, counts, x4, W, B, out, sc):
+def setup(pos, counts, sc):
     sec, gy, gx = pos
     nsec, ngy, ngx = counts
     lane = lax.broadcasted_iota(jnp.int32, (1, 128), 1)
@@ -50,12 +50,23 @@
             rb, lb = (right, left) if vb else (zero, zero)
             e = jnp.where(lane < 32, ra, jnp.where(lane < 64, lb, jnp.where(lane < 96, rb, la)))
             sc.emask[2 * va + vb] = e.astype(BF)
-
+    sc.xf[0:PAD] = jnp.zeros((PAD, 128), F32)
+    sc.xf[PAD + R12 :] = jnp.zeros((PAD, 128), F32)
+    sc.pf[:, 0:PAD] = jnp.zeros((14, PAD, 128), F32)
+    sc.pf[:, PAD + R12 :] = jnp.zeros((14, PAD, 128), F32)
+    sc.qf[:, 0:PAD] = jnp.zeros((6, PAD, 128), F32)
+    sc.qf[:, PAD + R10 :] = jnp.zeros((6, PAD, 128), F32)
+    sc.lf[:, 0:PAD] = jnp.zeros((8, PAD, 128), F32)
+    sc.lf[:, PAD + R8 :] = jnp.zeros((8, PAD, 128), F32)
+
+
+def compute(pos, counts, x4, W, B, out, sc):
+    sec, gy, gx = pos
+    nsec, ngy, ngx = counts
+    lane = lax.broadcasted_iota(jnp.int32, (1, 128), 1)
     def rowok(row, total):
         return jnp.where(jnp.logical_and(row >= 0, row < total), 1, 0)
 
-    sc.xf[0:PAD] = jnp.zeros((PAD, 128), F32)
-    sc.xf[PAD + R12 :] = jnp.zeros((PAD, 128), F32)
     for z in range(NZ):
         sc.xf[PAD + z * PITCH : PAD + (z + 1) * PITCH] = x4[z, 0:PITCH].astype(F32)
     sc.xin[:, 0:128] = sc.xf[PAD : PAD + R12].astype(BF)
@@ -81,8 +92,6 @@
         v = ref[(pl.ds(start, count),) + rest]
         return v.reshape(count * v.shape[1], v.shape[2])
 
-    sc.pf[:, 0:PAD] = jnp.zeros((14, PAD, 128), F32)
-    sc.pf[:, PAD + R12 :] = jnp.zeros((14, PAD, 128), F32)
 
     NP = OUTER_GROUP
 
@@ -116,8 +125,6 @@
 
     lax.fori_loop(0, 14 // NP, outer, 0)
 
-    sc.qf[:, 0:PAD] = jnp.zeros((6, PAD, 128), F32)
-    sc.qf[:, PAD + R10 :] = jnp.zeros((6, PAD, 128), F32)
 
     NK = INNER_GROUP
 
@@ -161,8 +168,6 @@
 
     lax.fori_loop(0, 6 // NK, inner, 0)
 
-    sc.lf[:, 0:PAD] = jnp.zeros((8, PAD, 128), F32)
-    sc.lf[:, PAD + R8 :] = jnp.zeros((8, PAD, 128), F32)
 
     pieces = []
     for dz in range(3):
@@ -771,9 +776,10 @@
         prep_plane(R["mend"], W["mend"], 64, ps)
         prep_plane(R["finish"], W["finish"], 32, ps)
         prep_head(R, W)
+        setup(axis_position(), counts, sc)
         finish()
+        compute(axis_position(), counts, cs.rx, W, B, out, sc)
         drain()
-        compute(axis_position(), counts, cs.rx, W, B, out, sc)
 
     dma = pltpu.SemaphoreType.DMA
     scratch = list(CS.values()) + list(SCRATCH.values()) + list(PS.values()) + list(WS.values())

time: 43.6 us -> 43.3 us (level)
  no operation moved by 1% of the time
where the time goes in v4:
time: 43.3 us; the launch traced here: 43.1 us
  Pallas kernels  41.5 us (96%)
  other arithmetic  1.64 us (4%)
    pallas_call x1, Pallas kernels, fused_call(): pl.pallas_call(body, out_shape=jax.ShapeDtypeStruct((3, 8, 8, 128), F32),...  41.5 us
    div x1, other arithmetic, per_device(): return jax.nn.sigmoid(logits + w['head_bias'][:, None, None, None])  1.64 us

profile of v4, /device:TPU:31, one launch (start us, length us, event | category | flops | bytes accessed | tf_op | source)
XLA Modules:
  0.0 43.1 jit_solution(5918161867703492891)
XLA Ops:
  0.0 0.0 copy-start
  0.0 41.5 %shard_map.226 = f32[3,8,8,128]{3,2,1,0:T(8,128)} custom-call(bf16[64,128]{1,0:T(8,128)(2,1)} %bitcast.45, s32[2,8]{1,0:T(2,128)} %bitcast.47, bf16[3,3,32]{2,1,0:T(4,128)(2,1)} %bitcast.46, bf16[3,3,32,32]{3,2,1,0:T(8,128)(2,1)} %bitcast.39, bf16[32,2,2,64]{3,2,1,0:T(2,128)(2,1)} %bitcast.43, bf16[3,3,3,4096]{3,2,1,0:T(4,128)(2,1)} %refs_5_.1, ...), custom_call_target="tpu_custom_call" | custom-call | tf_op jit(solution)/shard_map/pallas_call | solution.py:788
  41.5 0.0 copy-done
  41.5 1.6 %add_divide_fusion = f32[3,8,8,128]{3,2,1,0:T(8,128)} fusion(f32[3,8,8,128]{3,2,1,0:T(8,128)} %shard_map.226, f32[3]{0:T(128)S(1)} %copy-done), kind=kLoop, calls=%fused_computation | loop fusion | flops 98304 | bytes 196620 | tf_op jit(solution)/shard_map/div | solution.py:817
Async XLA Ops:
  0.0 41.5 %copy-start = (f32[3]{0:T(128)S(1)}, f32[3]{0:T(128)}, u32[]{:S(2)}) copy-start(f32[3]{0:T(128)} %param.47) | copy-start | bytes 40
